TPU v7x, 128 devices: a whole 4x4x4 slice. The times are simulated.
128 devices in a mesh: row: 16 (over x, y), col: 8 (over z, core).
Axes of the slice: x: 4, y: 4, z: 4, core: 2. Of those that a mesh axis runs over, the one named last changes fastest.
Arguments:
- amplitudes: bfloat16 [4, 4608, 4608], P(None, 'row', 'col'), may hold values from -6 to 6
- integrals: bfloat16 [4, 4608, 4608], P(None, 'col', 'row'), may hold values from -0.09375 to 0.09375
- pair_energy: float32 [4, 4608], replicated, may hold values from 0.5 to 3
- block_len: int32 [4, 8], replicated, may hold values from 1 to 576, 4032 in all within a row
Outputs:
- update: float32 [4, 4608, 4608], P(None, ('row', 'col'))
Inputs may be any that keep to these rules, and one draw needn't show every extreme that they name: `block_len`: each slice's block lengths sum to 4032; some block of every slice is full.
All inputs are finite; a program needn't handle non-finite values.
Results may differ from a plain program's by a relative error of at most 0.015.
Values may be sent and summed in bfloat16 or wider, within the bound.
A program may use at most 128 MiB of HBM per device.

v0:
```python
import jax
import jax.numpy as jnp
from jax import lax
from jax.sharding import PartitionSpec as P


def pair_live(lengths, npairs):
    capacity = npairs // 8
    position = jnp.arange(npairs, dtype=jnp.int32)
    irrep_of = position // capacity
    onehot = (irrep_of[:, None] == jnp.arange(8, dtype=jnp.int32)[None, :]).astype(jnp.int32)
    limits = jnp.sum(onehot * lengths[None, :], axis=1)
    return (position % capacity < limits).astype(jnp.float32)


def to_wire(values):
    rounded = lax.optimization_barrier(values.astype(jnp.bfloat16))
    return rounded.astype(jnp.float32)


def body(amplitudes, integrals, pair_energy, block_len):
    count = amplitudes.shape[0]
    rows_here = amplitudes.shape[1]
    cols_here = amplitudes.shape[2]
    npairs = pair_energy.shape[1]
    n_cols = lax.axis_size("col")
    row_index = lax.axis_index("row")
    col_index = lax.axis_index("col")
    share_rows = rows_here // n_cols
    row_start = (row_index * n_cols + col_index) * share_rows
    results = []
    for which in range(count):
        live = pair_live(block_len[which], npairs)
        live_sum = lax.dynamic_slice_in_dim(live, col_index * cols_here, cols_here)
        masked = amplitudes[which] * live_sum.astype(jnp.bfloat16)[None, :]
        coupling = integrals[which]
        partial_value = jnp.dot(
            masked,
            lax.all_gather(coupling, "row", axis=1, tiled=True),
            preferred_element_type=jnp.float32,
        )
        cycle_rows = lax.psum_scatter(
            to_wire(partial_value).astype(jnp.bfloat16), "col", scatter_dimension=0, tiled=True
        )
        received = lax.all_to_all(
            cycle_rows, ("row", "col"), split_axis=1, concat_axis=0, tiled=True
        )
        cycle_turned = received.T.astype(jnp.float32)
        cycle_here = cycle_rows.astype(jnp.float32)
        live_rows = lax.dynamic_slice_in_dim(live, row_start, share_rows)
        energy = pair_energy[which]
        energy_rows = lax.dynamic_slice_in_dim(energy, row_start, share_rows)
        scaled = (cycle_here + cycle_turned) / (energy_rows[:, None] + energy[None, :])
        results.append(live_rows[:, None] * live[None, :] * scaled)
    return jnp.stack(results)


def solution(mesh):
    return jax.shard_map(
        body,
        mesh=mesh,
        in_specs=(P(None, "row", "col"), P(None, "col", "row"), P(), P()),
        out_specs=P(None, ("row", "col"), None),
        check_vma=False,
    )
```

profile of v0, /device:TPU:1, one launch (start us, length us, event | category | flops | bytes accessed | tf_op | source)
XLA Modules:
  0.0 480.9 jit_solution(1878195103099747063)
XLA Ops:
  6.5 2.6 fusion.46
  12.2 60.0 %all-gather.9.cloned.1.call-done = bf16[1,576,4608]{1,2,0:T(8,128)(2,1)} async-done(((bf16[1,576,288]{1,2,0:T(8,128)(2,1)}), bf16[1,576,4608]{1,2,0:T(8,128)(2,1)}) %all-gather.9.cloned.1.call-update) | async-done | bytes 5308432 | tf_op jit(solution)/shard_map/all_gather | solution.py:39
  72.2 6.5 %convolution_convert_fusion.3 = bf16[288,4608]{1,0:T(8,128)(2,1)} fusion(bf16[1,576,4608]{1,2,0:T(8,128)(2,1)} %all-gather.9.cloned.1.call-done, bf16[4,288,576]{2,1,0:T(8,128)(2,1)S(1)} %copy-done.16, bf16[576]{0:T(1024)(128)(2,1)S(1)} %dynamic_slice.67), kind=kOutput, calls=%fused_computation.3 | convolution fusion | flops 1530316800 | bytes 8333312 | tf_op jit(solution)/shard_map/dot_general | solution.py:37
  78.7 54.8 %all-gather.11.cloned.1.call-done = bf16[1,576,4608]{1,2,0:T(8,128)(2,1)} async-done(((bf16[1,576,288]{1,2,0:T(8,128)(2,1)}), bf16[1,576,4608]{1,2,0:T(8,128)(2,1)}) %all-gather.11.cloned.1.call-update) | async-done | bytes 5308432 | tf_op jit(solution)/shard_map/all_gather | solution.py:39
  133.5 6.4 %convolution_convert_fusion.2 = bf16[288,4608]{1,0:T(8,128)(2,1)} fusion(bf16[1,576,4608]{1,2,0:T(8,128)(2,1)} %all-gather.11.cloned.1.call-done, bf16[4,288,576]{2,1,0:T(8,128)(2,1)S(1)} %copy-done.16, bf16[576]{0:T(1024)(128)(2,1)S(1)} %dynamic_slice.66), kind=kOutput, calls=%fused_computation.2 | convolution fusion | flops 1530316800 | bytes 8333312 | tf_op jit(solution)/shard_map/dot_general | solution.py:37
  139.9 54.9 %all-gather.13.cloned.1.call-done = bf16[1,576,4608]{1,2,0:T(8,128)(2,1)} async-done(((bf16[1,576,288]{1,2,0:T(8,128)(2,1)}), bf16[1,576,4608]{1,2,0:T(8,128)(2,1)}) %all-gather.13.cloned.1.call-update) | async-done | bytes 5308432 | tf_op jit(solution)/shard_map/all_gather | solution.py:39
  194.8 6.4 %convolution_convert_fusion.1 = bf16[288,4608]{1,0:T(8,128)(2,1)} fusion(bf16[1,576,4608]{1,2,0:T(8,128)(2,1)} %all-gather.13.cloned.1.call-done, bf16[4,288,576]{2,1,0:T(8,128)(2,1)S(1)} %copy-done.16, bf16[576]{0:T(1024)(128)(2,1)S(1)} %dynamic_slice.65), kind=kOutput, calls=%fused_computation.1 | convolution fusion | flops 1530316800 | bytes 8333312 | tf_op jit(solution)/shard_map/dot_general | solution.py:37
  201.2 54.7 %all-gather.15.cloned.1.call-done = bf16[1,576,4608]{1,2,0:T(8,128)(2,1)} async-done(((bf16[1,576,288]{1,2,0:T(8,128)(2,1)}), bf16[1,576,4608]{1,2,0:T(8,128)(2,1)}) %all-gather.15.cloned.1.call-update) | async-done | bytes 5308432 | tf_op jit(solution)/shard_map/all_gather | solution.py:39
  256.0 6.4 %convolution_convert_fusion = bf16[288,4608]{1,0:T(8,128)(2,1)} fusion(bf16[1,576,4608]{1,2,0:T(8,128)(2,1)} %all-gather.15.cloned.1.call-done, bf16[4,288,576]{2,1,0:T(8,128)(2,1)S(1)} %copy-done.16, bf16[576]{0:T(1024)(128)(2,1)S(1)} %dynamic_slice.64), kind=kOutput, calls=%fused_computation | convolution fusion | flops 1530316800 | bytes 8333312 | tf_op jit(solution)/shard_map/dot_general | solution.py:37
  262.4 69.1 %fusion.45 = (bf16[40,4608]{1,0:T(8,128)(2,1)S(1)}, bf16[40,4608]{1,0:T(8,128)(2,1)S(1)}, bf16[40,4608]{1,0:T(8,128)(2,1)S(1)}, bf16[40,4608]{1,0:T(8,128)(2,1)S(1)}) fusion(bf16[288,4608]{1,0:T(8,128)(2,1)} %convolution_convert_fusion, bf16[288,4608]{1,0:T(8,128)(2,1)} %convolution_convert_fusion.1, bf16[288,4608]{1,0:T(8,128)(2,1)} %convolution_convert_fusion.2, ...), kind=kCustom, calls=%all-reduce-scatter.4 | all-reduce-scatter fusion | flops 5898241 | bytes 12091904
  331.6 4.4 collective-permute-start
  338.6 1.9 collective-permute-start.1
  341.3 3.3 collective-permute-start.2
  345.3 2.1 collective-permute-start.3
  348.1 0.8 constant_dynamic-slice_fusion.3
  348.9 4.2 all_to_all.40
  353.9 2.4 reshape.110
  356.3 6.6 %all-to-all-start = ((bf16[128,2,648]{2,1,0:T(2,128)(2,1)}), bf16[128,2,648]{2,1,0:T(2,128)(2,1)}, u32[]{:S(2)}, u32[]{:S(2)}) async-start(bf16[128,2,648]{2,1,0:T(2,128)(2,1)} %reshape.110), calls=%async_computation | async-start | bytes 786432 | tf_op jit(solution)/shard_map/all_to_all | solution.py:45
  363.0 2.4 concatenate.1
  366.2 3.1 all_to_all.42
  370.1 2.4 reshape.108
  372.5 4.7 concatenate.2
  377.3 10.6 %all-to-all-start.1 = ((bf16[128,2,648]{2,1,0:T(2,128)(2,1)}), bf16[128,2,648]{2,1,0:T(2,128)(2,1)}, u32[]{:S(2)}, u32[]{:S(2)}) async-start(bf16[128,2,648]{2,1,0:T(2,128)(2,1)} %reshape.108), calls=%async_computation.1 | async-start | bytes 786432 | tf_op jit(solution)/shard_map/all_to_all | solution.py:45
  387.9 3.1 all_to_all.44
  391.9 2.4 reshape.106
  394.3 4.7 concatenate.3
  399.6 9.6 %all-to-all-start.2 = ((bf16[128,2,648]{2,1,0:T(2,128)(2,1)}), bf16[128,2,648]{2,1,0:T(2,128)(2,1)}, u32[]{:S(2)}, u32[]{:S(2)}) async-start(bf16[128,2,648]{2,1,0:T(2,128)(2,1)} %reshape.106), calls=%async_computation.2 | async-start | bytes 786432 | tf_op jit(solution)/shard_map/all_to_all | solution.py:45
  409.3 3.1 all_to_all.46
  413.2 2.4 reshape.104
  415.6 3.7 reshape.111
  419.4 3.8 reshape.109
  423.1 1.5 convert_bitcast_fusion.3
  424.6 10.6 %all-to-all-start.3 = ((bf16[128,2,648]{2,1,0:T(2,128)(2,1)}), bf16[128,2,648]{2,1,0:T(2,128)(2,1)}, u32[]{:S(2)}, u32[]{:S(2)}) async-start(bf16[128,2,648]{2,1,0:T(2,128)(2,1)} %reshape.104), calls=%async_computation.3 | async-start | bytes 786432 | tf_op jit(solution)/shard_map/all_to_all | solution.py:45
  435.2 3.0 convert_bitcast_fusion.2
  438.2 1.5 reshape.92
  439.7 3.4 copy.33
  443.1 1.5 reshape.93
  444.6 3.3 copy.34
  447.9 3.7 reshape.107
  451.6 1.5 convert_bitcast_fusion.1
  453.1 1.5 reshape.94
  454.6 3.2 copy.35
  457.8 3.7 reshape.105
  461.6 1.5 convert_bitcast_fusion
  463.1 1.5 reshape.95
  464.6 3.3 copy.36
  467.9 2.0 fusion.16
  470.7 3.2 copy.32
  (85 shorter events, 12.8 us)
Async XLA Ops:
  6.5 4.7 copy-start.14
  6.5 5.4 %copy-start.13 = (f32[4,4608]{1,0:T(4,128)S(1)}, f32[4,4608]{1,0:T(4,128)}, u32[]{:S(2)}) copy-start(f32[4,4608]{1,0:T(4,128)} %param.6) | copy-start | bytes 221188
  6.5 65.6 %copy-start.16 = (bf16[4,288,576]{2,1,0:T(8,128)(2,1)S(1)}, bf16[4,288,576]{2,1,0:T(8,128)(2,1)}, u32[]{:S(2)}) copy-start(bf16[4,288,576]{2,1,0:T(8,128)(2,1)} %param.4) | copy-start | bytes 3981316
  6.5 65.6 %all-gather.9.cloned.1.call-start = ((), (), s32[]{:S(2)}) async-start(), calls=%async_computation.4 | async-start | bytes 6266880 | tf_op jit(solution)/shard_map/all_gather | solution.py:39
  9.1 124.3 %all-gather.11.cloned.1.call-start = ((), (), s32[]{:S(2)}) async-start(), calls=%async_computation.5 | async-start | bytes 6266880 | tf_op jit(solution)/shard_map/all_gather | solution.py:39
  9.9 184.9 %all-gather.13.cloned.1.call-start = ((), (), s32[]{:S(2)}) async-start(), calls=%async_computation.6 | async-start | bytes 6266880 | tf_op jit(solution)/shard_map/all_gather | solution.py:39
  10.6 245.3 %all-gather.15.cloned.1.call-start = ((), (), s32[]{:S(2)}) async-start(), calls=%async_computation.7 | async-start | bytes 6266880 | tf_op jit(solution)/shard_map/all_gather | solution.py:39
  262.4 74.0 %copy-start.15 = (u32[128]{0:T(128)S(1)}, u32[128]{0:T(128)}, u32[]{:S(2)}) copy-start(u32[128]{0:T(128)} %constant.61) | copy-start | bytes 1540
  331.5 17.4 %copy-start.9 = (bf16[40,4608]{1,0:T(8,128)(2,1)}, bf16[40,4608]{1,0:T(8,128)(2,1)S(1)}, u32[]{:S(2)}) copy-start(bf16[40,4608]{1,0:T(8,128)(2,1)S(1)} %get-tuple-element.17) | copy-start | bytes 1105924
  331.5 17.4 %copy-start.10 = (bf16[40,4608]{1,0:T(8,128)(2,1)}, bf16[40,4608]{1,0:T(8,128)(2,1)S(1)}, u32[]{:S(2)}) copy-start(bf16[40,4608]{1,0:T(8,128)(2,1)S(1)} %get-tuple-element.18) | copy-start | bytes 1105924
  331.5 17.4 %copy-start.11 = (bf16[40,4608]{1,0:T(8,128)(2,1)}, bf16[40,4608]{1,0:T(8,128)(2,1)S(1)}, u32[]{:S(2)}) copy-start(bf16[40,4608]{1,0:T(8,128)(2,1)S(1)} %get-tuple-element.19) | copy-start | bytes 1105924
  331.6 15.8 %collective-permute-start = (bf16[28,4608]{1,0:T(8,128)(2,1)S(1)}, bf16[28,4608]{1,0:T(8,128)(2,1)S(1)}, u32[]{:S(2)}, u32[]{:S(2)}) collective-permute-start(bf16[28,4608]{1,0:T(8,128)(2,1)S(1)} %slice.64), channel_id=1, source_target_pairs={{0,1},{1,2},{2,3},{3,4},{4,5},{5,6},{6,7},{8,9},{9,10},{10,11},{11... | collective-permute-start | bytes 774152
  338.6 24.4 %collective-permute-start.1 = (bf16[28,4608]{1,0:T(8,128)(2,1)}, bf16[28,4608]{1,0:T(8,128)(2,1)}, u32[]{:S(2)}, u32[]{:S(2)}) collective-permute-start(bf16[28,4608]{1,0:T(8,128)(2,1)} %slice.65), channel_id=1, source_target_pairs={{0,1},{1,2},{2,3},{3,4},{4,5},{5,6},{6,7},{8,9},{9,10},{10,11},{11... | collective-permute-start | bytes 774152
  341.3 31.2 %collective-permute-start.2 = (bf16[28,4608]{1,0:T(8,128)(2,1)}, bf16[28,4608]{1,0:T(8,128)(2,1)}, u32[]{:S(2)}, u32[]{:S(2)}) collective-permute-start(bf16[28,4608]{1,0:T(8,128)(2,1)} %slice.66), channel_id=1, source_target_pairs={{0,1},{1,2},{2,3},{3,4},{4,5},{5,6},{6,7},{8,9},{9,10},{10,11},{11... | collective-permute-start | bytes 774152
  345.3 48.9 %collective-permute-start.3 = (bf16[28,4608]{1,0:T(8,128)(2,1)}, bf16[28,4608]{1,0:T(8,128)(2,1)}, u32[]{:S(2)}, u32[]{:S(2)}) collective-permute-start(bf16[28,4608]{1,0:T(8,128)(2,1)} %slice.67), channel_id=1, source_target_pairs={{0,1},{1,2},{2,3},{3,4},{4,5},{5,6},{6,7},{8,9},{9,10},{10,11},{11... | collective-permute-start | bytes 774152
  353.9 9.0 %copy-start.12 = (bf16[40,4608]{1,0:T(8,128)(2,1)S(1)}, bf16[40,4608]{1,0:T(8,128)(2,1)}, u32[]{:S(2)}) copy-start(bf16[40,4608]{1,0:T(8,128)(2,1)} %copy-done.11) | copy-start | bytes 1105924
  356.3 20.9 %all-to-all-start = ((bf16[128,2,648]{2,1,0:T(2,128)(2,1)}), bf16[128,2,648]{2,1,0:T(2,128)(2,1)}, u32[]{:S(2)}, u32[]{:S(2)}) async-start(bf16[128,2,648]{2,1,0:T(2,128)(2,1)} %reshape.110), calls=%async_computation | async-start | bytes 786432 | tf_op jit(solution)/shard_map/all_to_all | solution.py:45
  365.3 0.9 copy-start.3
  377.2 10.7 %copy-start.1 = (bf16[68,4608]{1,0:T(8,128)(2,1)}, bf16[68,4608]{1,0:T(8,128)(2,1)S(1)}, u32[]{:S(2)}) copy-start(bf16[68,4608]{1,0:T(8,128)(2,1)S(1)} %concatenate.2) | copy-start | bytes 1880068
  377.3 22.3 %all-to-all-start.1 = ((bf16[128,2,648]{2,1,0:T(2,128)(2,1)}), bf16[128,2,648]{2,1,0:T(2,128)(2,1)}, u32[]{:S(2)}, u32[]{:S(2)}) async-start(bf16[128,2,648]{2,1,0:T(2,128)(2,1)} %reshape.108), calls=%async_computation.1 | async-start | bytes 786432 | tf_op jit(solution)/shard_map/all_to_all | solution.py:45
  399.0 10.3 %copy-start.5 = (bf16[68,4608]{1,0:T(8,128)(2,1)}, bf16[68,4608]{1,0:T(8,128)(2,1)S(1)}, u32[]{:S(2)}) copy-start(bf16[68,4608]{1,0:T(8,128)(2,1)S(1)} %concatenate.3) | copy-start | bytes 1880068
  399.6 25.0 %all-to-all-start.2 = ((bf16[128,2,648]{2,1,0:T(2,128)(2,1)}), bf16[128,2,648]{2,1,0:T(2,128)(2,1)}, u32[]{:S(2)}, u32[]{:S(2)}) async-start(bf16[128,2,648]{2,1,0:T(2,128)(2,1)} %reshape.106), calls=%async_computation.2 | async-start | bytes 786432 | tf_op jit(solution)/shard_map/all_to_all | solution.py:45
  424.6 33.2 %all-to-all-start.3 = ((bf16[128,2,648]{2,1,0:T(2,128)(2,1)}), bf16[128,2,648]{2,1,0:T(2,128)(2,1)}, u32[]{:S(2)}, u32[]{:S(2)}) async-start(bf16[128,2,648]{2,1,0:T(2,128)(2,1)} %reshape.104), calls=%async_computation.3 | async-start | bytes 786432 | tf_op jit(solution)/shard_map/all_to_all | solution.py:45
  439.7 3.4 copy-start
  464.6 3.3 copy-start.4
  467.9 2.0 copy-start.2
  467.9 2.0 copy-start.6
  467.9 2.0 copy-start.7
  467.9 2.2 copy-start.8
Sparse Core Ops, SparseCore 0:
  9.5 62.5 all-gather.8
  74.4 59.0 all-gather.10
  135.7 59.0 all-gather.12
  196.8 59.0 all-gather.14
where the time goes:
time: 490 us; the launch traced here: 481 us
  waiting for transfers between devices  227 us (46%)
  local copies, waits for them, and re-layouts  84.9 us (17%)
  blocking collectives  69.1 us (14%)
  starting transfers between devices  49.1 us (10%)
  matrix products  25.8 us (5%)
  between operations  14.7 us (3%)
  other arithmetic  10.4 us (2%)
    all_gather x4, waiting for transfers between devices, body(): lax.all_gather(coupling, 'row', axis=1, tiled=True)  224 us
    unnamed x1, blocking collectives  69.1 us
    unnamed x55, local copies, waits for them, and re-layouts  42.1 us
    all_to_all x4, starting transfers between devices, body(): lax.all_to_all(cycle_rows, ('row', 'col'), split_axis=1, concat_axis=0, t...  37.4 us
    dot_general x4, matrix products, body(): jnp.dot(masked, lax.all_gather(coupling, 'row', axis=1, tiled=True), pref...  25.8 us
    convert_element_type x8, local copies, waits for them, and re-layouts, body(): cycle_turned = received.T.astype(jnp.float32)  19.2 us
    all_to_all x8, local copies, waits for them, and re-layouts, body(): lax.all_to_all(cycle_rows, ('row', 'col'), split_axis=1, concat_axis=0, t...  16.7 us
    unnamed x4, starting transfers between devices  11.6 us
  transfers between devices with their start and end apart: 12, of which 5 were waited for; matrix products, arithmetic and copies ran while one was open for 17% of the time, Pallas kernels for 0%

commit v1 on v0

v1 whole, which is shorter than its diff:
```python
import functools

import jax
import jax.numpy as jnp
from jax import lax
from jax.experimental import pallas as pl
from jax.experimental.pallas import tpu as pltpu
from jax.sharding import PartitionSpec as P

MESH = pl.DeviceIdType.MESH
BF = jnp.bfloat16
F32 = jnp.float32
I32 = jnp.int32


def nt(a, b):
    return lax.dot_general(a, b, (((1,), (1,)), ((), ())), preferred_element_type=F32)


def nn(a, b):
    return jnp.dot(a, b, preferred_element_type=F32)


def iota(shape, dim):
    return lax.broadcasted_iota(I32, shape, dim)


def natural(j):
    return 2 * (j & 3) + (j >> 2)


def kernel(
    a_hbm, b_hbm, e_ref, l_ref, o_hbm,
    av, bv, ga, gb, rg, ps, cx, pf, q1, q2, z1a, z1b, z2, own, db, hh, txm, txr,
    um, ur, tm, tr, tt, pm, eye, qp, sel, s1, s2, mk, er, ob,
    lsem, g1s, g1r, g2s, g2r, cs, cr, z1s, z1r, z2s, z2r, hs, hr, xs, xr, ts, tsr, osem,
):
    row = lax.axis_index("row")
    col = lax.axis_index("col")
    x, y = row // 4, row % 4
    z, c = col // 2, col % 2
    jme = c * 4 + z

    def at(dx, dy, dz, dc):
        return ((x + dx) % 4 * 4 + (y + dy) % 4, (z + dz) % 4 * 2 + (c + dc) % 2)

    def remote(src, dst, ssem, rsem, where):
        return pltpu.make_async_remote_copy(
            src_ref=src, dst_ref=dst, send_sem=ssem, recv_sem=rsem, device_id=where, device_id_type=MESH
        )

    def load(s):
        return (
            pltpu.make_async_copy(a_hbm.at[s], av.at[s], lsem.at[s, 0]),
            pltpu.make_async_copy(b_hbm.at[s], bv.at[s], lsem.at[s, 1]),
        )

    for s in range(4):
        for cp in load(s):
            cp.start()

    def rows_of(v, size):
        return pl.ds(pl.multiple_of(v * size, size), size)

    def gather1(s):
        out = []
        for d, step in ((0, 1), (1, 3)):
            to_y, to_x = at(0, step, 0, 0), at(step, 0, 0, 0)
            main = ga.at[s, :, rows_of(y, 32), :]
            out.append(remote(main, main, g1s.at[s, d, 0], g1r.at[s, d, 0], to_y))
            rem = rg.at[s, y]
            out.append(remote(rem, rem, g1s.at[s, d, 1], g1r.at[s, d, 1], to_y))
            blk = gb.at[s, rows_of(x, 288), :]
            out.append(remote(blk, blk, g1s.at[s, d, 2], g1r.at[s, d, 2], to_x))
        return out

    def gather2(s):
        out = []
        for d, step in ((0, 1), (1, 3)):
            to_y, to_x = at(0, step, 0, 0), at(step, 0, 0, 0)
            ysrc, xsrc = (y + 4 - step) % 4, (x + 4 - step) % 4
            main = ga.at[s, pl.ds(4 * d, 4), rows_of(ysrc, 32), :]
            out.append(remote(main, main, g2s.at[s, d, 0], g2r.at[s, d, 0], to_y))
            rem = rg.at[s, ysrc, pl.ds(16 * d, 16), :]
            out.append(remote(rem, rem, g2s.at[s, d, 1], g2r.at[s, d, 1], to_y))
            blk = gb.at[s, pl.ds(pl.multiple_of(xsrc * 288 + 144 * d, 16), 144), :]
            out.append(remote(blk, blk, g2s.at[s, d, 2], g2r.at[s, d, 2], to_x))
        return out

    def swap(s):
        return [remote(ps.at[s], cx.at[s], cs.at[s], cr.at[s], at(0, 0, 0, 1))]

    def zstep1(s):
        return [
            remote(q1.at[s, pl.ds(0, 80), :], z1a.at[s], z1s.at[s, 0], z1r.at[s, 0], at(0, 0, 1, 0)),
            remote(q1.at[s, pl.ds(80, 64), :], z1b.at[s], z1s.at[s, 1], z1r.at[s, 1], at(0, 0, 3, 0)),
        ]

    def zstep2(s):
        return [
            remote(q2.at[s, d], z2.at[s, d], z2s.at[s, d], z2r.at[s, d], at(0, 0, step, 0))
            for d, step in ((0, 1), (1, 3))
        ]

    def here_copies(s):
        out = []
        for d in (1, 2, 3):
            to = at(0, d, 0, 0)
            out.append(remote(
                db.at[s, rows_of((y + d) % 4, 32), :], hh.at[s, y, pl.ds(0, 32), :],
                hs.at[s, d - 1, 0], hr.at[s, d - 1, 0], to,
            ))
            out.append(remote(
                db.at[s, pl.ds(128, 16), :], hh.at[s, y, pl.ds(32, 16), :],
                hs.at[s, d - 1, 1], hr.at[s, d - 1, 1], to,
            ))
        return out

    def turn_copies(s):
        out = []
        for d in (1, 2, 3):
            to = at(d, 0, 0, 0)
            lanes = pl.ds(pl.multiple_of((x + d) % 4 * 256, 256), 384)
            out.append(remote(
                db.at[s, pl.ds(0, 128), lanes], txm.at[s, rows_of(x, 128), :],
                xs.at[s, d - 1, 0], xr.at[s, d - 1, 0], to,
            ))
            out.append(remote(
                db.at[s, pl.ds(128, 16), lanes], txr.at[s, rows_of(x, 16), :],
                xs.at[s, d - 1, 1], xr.at[s, d - 1, 1], to,
            ))
        return out

    def last_copies(s):
        out = []
        for i in range(1, 8):
            dz, dc = i // 2, i % 2
            to = at(0, 0, dz, dc)
            jto = (c + dc) % 2 * 4 + (z + dz) % 4
            lanes = rows_of(jme, 128)
            out.append(remote(um.at[s, jto], tm.at[s, :, :, lanes], ts.at[s, i - 1, 0], tsr.at[s, i - 1, 0], to))
            out.append(remote(ur.at[s, jto], tr.at[s, :, lanes], ts.at[s, i - 1, 1], tsr.at[s, i - 1, 1], to))
        return out

    def result_copy(s):
        return pltpu.make_async_copy(ob.at[s], o_hbm.at[s], osem.at[s])

    def start(copies):
        for cp in copies:
            cp.start()

    def arrive(copies):
        for cp in copies:
            cp.wait_recv()

    def prepare(s):
        for cp in load(s):
            cp.wait()
        limit = l_ref[s, col]
        masked = jnp.where(iota((288, 576), 1) < limit, av[s].astype(F32), 0.0).astype(BF)
        turned = nn(pm[...], masked).astype(BF)
        ga[s, :, rows_of(y, 32), :] = turned[:256].reshape(8, 32, 576)
        rg[s, y] = turned[256:]
        gb[s, rows_of(x, 288), :] = nt(eye[...], bv[s]).astype(BF)

    def multiply(s):
        arrive(gather2(s))
        rest = nn(qp[...], rg[s].reshape(128, 576)).astype(BF)
        ga[s, :, 128:144, :] = rest.reshape(8, 16, 576)

        def other(n, _):
            cols = pl.ds(pl.multiple_of(n * 384, 384), 384)
            lhs = ga[s, pl.ds((1 - c) * 4, 4)].reshape(576, 576)
            ps[s, :, :, cols] = nt(lhs, gb[s, cols, :]).astype(BF).reshape(4, 144, 384)
            return 0

        lax.fori_loop(0, 3, other, 0)
        start(swap(s))

        def mine(n, _):
            cols = pl.ds(pl.multiple_of(n * 384, 384), 384)
            lhs = ga[s, pl.ds(c * 4, 4)].reshape(576, 576)
            pf[:, :, cols] = nt(lhs, gb[s, cols, :]).reshape(4, 144, 384)
            return 0

        lax.fori_loop(0, 3, mine, 0)

    def first_sum(s):
        arrive(swap(s))
        far = (z + 2) % 4

        def add(i, _):
            rows = rows_of(i, 16)
            q1[s, rows, :] = (pf[far, rows, :] + cx[s, far, rows, :].astype(F32)).astype(BF)
            return 0

        lax.fori_loop(0, 9, add, 0)
        start(zstep1(s))

    def second_sum(s):
        arrive(zstep1(s))
        up, down = (z + 1) % 4, (z + 3) % 4

        def add_low(i, _):
            rows = rows_of(i, 16)
            q2[s, 0, rows, :] = (
                pf[up, rows, :] + cx[s, up, rows, :].astype(F32) + z1a[s, rows, :].astype(F32)
            ).astype(BF)
            q2[s, 1, rows, :] = (pf[down, rows, :] + cx[s, down, rows, :].astype(F32)).astype(BF)
            return 0

        lax.fori_loop(0, 5, add_low, 0)

        def add_high(i, _):
            rows = pl.ds(pl.multiple_of(i * 16 + 80, 16), 16)
            got = rows_of(i, 16)
            q2[s, 0, rows, :] = (pf[up, rows, :] + cx[s, up, rows, :].astype(F32)).astype(BF)
            q2[s, 1, rows, :] = (
                pf[down, rows, :] + cx[s, down, rows, :].astype(F32) + z1b[s, got, :].astype(F32)
            ).astype(BF)
            return 0

        lax.fori_loop(0, 4, add_high, 0)
        start(zstep2(s))

        def keep(i, _):
            rows = rows_of(i, 16)
            own[rows, :] = pf[z, rows, :] + cx[s, z, rows, :].astype(F32)
            return 0

        lax.fori_loop(0, 9, keep, 0)

    def whole_sum(s):
        arrive(zstep2(s))

        def add(i, _):
            rows = rows_of(i, 16)
            db[s, rows, :] = (own[rows, :] + z2[s, 0, rows, :].astype(F32) + z2[s, 1, rows, :].astype(F32)).astype(BF)
            return 0

        lax.fori_loop(0, 9, add, 0)
        start(turn_copies(s))
        start(here_copies(s))
        hh[s, y, 0:32, :] = db[s, rows_of(y, 32), :]
        hh[s, y, 32:48, :] = db[s, 128:144, :]
        lanes = pl.ds(pl.multiple_of(x * 256, 256), 384)
        txm[s, rows_of(x, 128), :] = db[s, 0:128, lanes]
        txr[s, rows_of(x, 16), :] = db[s, 128:144, lanes]

    def turn(s):
        arrive(turn_copies(s))
        main = nt(sel[...], txm[s]).astype(BF)
        for xx in range(4):
            um[s, :, xx] = main[:, 128 * xx:128 * xx + 128].reshape(8, 48, 128)
        rest = nt(sel[...], txr[s])
        rest = jnp.concatenate([rest, jnp.zeros_like(rest)], axis=1)
        ur[s] = rest.astype(BF).reshape(8, 48, 128)
        start(last_copies(s))
        lanes = rows_of(jme, 128)
        tm[s, :, :, lanes] = um[s, jme]
        tr[s, :, lanes] = ur[s, jme]

    def finish(s):
        arrive(last_copies(s))
        lhs = tm[s].reshape(192, 1024)
        rest = tr[s]
        rest = jnp.concatenate([rest * mk[16 * xx:16 * xx + 1, :] for xx in range(4)], axis=0)
        for n in range(3):
            cols = slice(384 * n, 384 * n + 384)
            tt[:, :, cols] = (nn(lhs, s1[:, cols]) + nn(rest, s2[:, cols])).reshape(4, 48, 384)
        arrive(here_copies(s))
        dev = row * 8 + col
        row_limit = l_ref[s, dev // 16] - (dev % 16) * 36
        row_live = (iota((36, 1), 0) < row_limit).astype(F32)
        row_energy = er[s, 0:36, 0:1]
        pieces = []
        for yy in range(4):
            part = hh[s, yy].astype(F32)
            low = pltpu.roll(part[32:48], (16 - 4 * y) % 16, 0)
            pieces.append(jnp.concatenate([part[:32], low[:8]], axis=0))
        lane = iota((1, 1152), 1)
        for xx in range(4):
            local = jnp.concatenate([p[:, 288 * xx:288 * xx + 288] for p in pieces], axis=1)
            total = local[:36] + tt[xx, 0:36, :]
            bound = jnp.where(lane < 576, l_ref[s, 2 * xx], l_ref[s, 2 * xx + 1] + 576)
            col_live = (lane < bound).astype(F32)
            energy = row_energy + e_ref[pl.ds(s, 1), 1152 * xx:1152 * xx + 1152]
            ob[s, :, 1152 * xx:1152 * xx + 1152] = row_live * col_live * total / energy
        result_copy(s).start()

    def early_constants():
        i = iota((288, 288), 0)
        k = iota((288, 288), 1)
        head = 36 * natural(i >> 5) + (i & 31)
        tail = 36 * natural((i - 256) >> 2) + 32 + (i & 3)
        pm[...] = (k == jnp.where(i < 256, head, tail)).astype(F32).astype(BF)
        eye[...] = (k == i).astype(F32).astype(BF)
        i = iota((128, 128), 0)
        k = iota((128, 128), 1)
        qp[...] = (k == 32 * ((i >> 2) & 3) + 4 * (i >> 4) + (i & 3)).astype(F32).astype(BF)

    def late_constants():
        j, t, k = (iota((8, 48, 384), n) for n in range(3))
        hit = (k == 32 * x + 36 * natural(j) + t) & (t < 36)
        sel[...] = hit.astype(F32).astype(BF).reshape(384, 384)

        def fill(j, _):
            rows = rows_of(j, 128)
            r = iota((128, 1152), 0)
            k = iota((128, 1152), 1)
            base = 36 * natural(j)
            s1[rows, :] = (k == 288 * (r >> 5) + base + (r & 31)).astype(F32).astype(BF)
            hit = (k == 288 * ((r >> 2) & 3) + base + 32 + (r & 3)) & (r < 64)
            s2[rows, :] = hit.astype(F32).astype(BF)
            return 0

        lax.fori_loop(0, 8, fill, 0)
        r = iota((64, 1024), 0)
        k = iota((64, 1024), 1)
        mk[...] = (((k & 127) >> 4) == (r >> 4)).astype(F32).astype(BF)
        dev = row * 8 + col
        pick = iota((40, 4608), 1) == iota((40, 4608), 0) + dev * 36
        for s in range(4):
            got = jnp.sum(jnp.where(pick, e_ref[s:s + 1, :], 0.0), axis=1, keepdims=True)
            er[s] = jnp.broadcast_to(got, (40, 128))

    early_constants()
    prepare(0)
    barrier = pltpu.get_barrier_semaphore()
    partners = [at(d, 0, 0, 0) for d in (1, 2, 3)] + [at(0, d, 0, 0) for d in (1, 2, 3)]
    partners += [at(0, 0, i // 2, i % 2) for i in range(1, 8)]
    for p in partners:
        pl.semaphore_signal(barrier, 1, device_id=p, device_id_type=MESH)
    pl.semaphore_wait(barrier, len(partners))
    start(gather1(0))
    late_constants()

    def during(r, low, high, what):
        @pl.when((r >= low) & (r < high))
        def _():
            what(r - low)

    def forward(s):
        arrive(gather1(s))
        start(gather2(s))

    def one_round(r, _):
        during(r, 0, 3, lambda s: prepare(s + 1))
        during(r, 0, 4, forward)
        during(r, 0, 3, lambda s: start(gather1(s + 1)))
        during(r, 1, 5, second_sum)
        during(r, 2, 6, turn)
        during(r, 0, 4, multiply)
        during(r, 0, 4, first_sum)
        during(r, 1, 5, whole_sum)
        during(r, 2, 6, finish)
        return 0

    lax.fori_loop(0, 6, one_round, 0)

    def drain(s, _):
        for copies in (gather1, gather2, swap, zstep1, zstep2, here_copies, turn_copies, last_copies):
            for cp in copies(s):
                cp.wait_send()
        result_copy(s).wait()
        return 0

    lax.fori_loop(0, 4, drain, 0)


def body(amplitudes, integrals, pair_energy, block_len):
    bf = lambda *shape: pltpu.VMEM(shape, BF)
    f32 = lambda *shape: pltpu.VMEM(shape, F32)
    dma = lambda *shape: pltpu.SemaphoreType.DMA(shape)
    scratch = [
        bf(4, 288, 576), bf(4, 576, 288),
        bf(4, 8, 144, 576), bf(4, 1152, 576), bf(4, 4, 32, 576),
        bf(4, 4, 144, 1152), bf(4, 4, 144, 1152), f32(4, 144, 1152),
        bf(4, 144, 1152), bf(4, 2, 144, 1152),
        bf(4, 80, 1152), bf(4, 64, 1152), bf(4, 2, 144, 1152),
        f32(144, 1152), bf(4, 144, 1152),
        bf(4, 4, 48, 1152), bf(4, 512, 384), bf(4, 64, 384),
        bf(4, 8, 4, 48, 128), bf(4, 8, 48, 128), bf(4, 4, 48, 1024), bf(4, 48, 1024),
        f32(4, 48, 1152),
        bf(288, 288), bf(288, 288), bf(128, 128), bf(384, 384), bf(1024, 1152), bf(1024, 1152), bf(64, 1024),
        f32(4, 40, 128), f32(4, 36, 4608),
        dma(4, 2), dma(4, 2, 3), dma(4, 2, 3), dma(4, 2, 3), dma(4, 2, 3), dma(4), dma(4),
        dma(4, 2), dma(4, 2), dma(4, 2), dma(4, 2),
        dma(4, 3, 2), dma(4, 3, 2), dma(4, 3, 2), dma(4, 3, 2), dma(4, 7, 2), dma(4, 7, 2), dma(4),
    ]
    count, npairs = pair_energy.shape
    return pl.pallas_call(
        kernel,
        out_shape=jax.ShapeDtypeStruct((count, npairs // 128, npairs), F32),
        in_specs=[
            pl.BlockSpec(memory_space=pl.ANY),
            pl.BlockSpec(memory_space=pl.ANY),
            pl.BlockSpec(memory_space=pltpu.VMEM),
            pl.BlockSpec(memory_space=pltpu.SMEM),
        ],
        out_specs=pl.BlockSpec(memory_space=pl.ANY),
        scratch_shapes=scratch,
        compiler_params=pltpu.CompilerParams(
            collective_id=0, has_side_effects=True, vmem_limit_bytes=63 << 20
        ),
        name="cycle",
    )(amplitudes, integrals, pair_energy, block_len)


def solution(mesh):
    return jax.shard_map(
        body,
        mesh=mesh,
        in_specs=(P(None, "row", "col"), P(None, "col", "row"), P(), P()),
        out_specs=P(None, ("row", "col"), None),
        check_vma=False,
    )
```

time: 490 us -> 131 us (0.27); the launches traced: 481 us -> 131 us
  waiting for transfers between devices: 227 us -> 0 us
  Pallas kernels: 0 us -> 122 us
  local copies, waits for them, and re-layouts: 84.9 us -> 8.54 us
  blocking collectives: 69.1 us -> 0 us
  starting transfers between devices: 49.1 us -> 0 us
  matrix products: 25.8 us -> 0 us
  between operations: 14.7 us -> 0.01 us
  other arithmetic: 10.4 us -> 0 us
    all_gather x4 -> x0, waiting for transfers between devices: 224 us -> none  [body(): lax.all_gather(coupling, 'row', axis=1, tiled=True)]
    pallas_call x0 -> x1, Pallas kernels: none -> 122 us  [body(): pl.pallas_call(kernel, out_shape=jax.ShapeDtypeStruct((count, npairs // 1...]
    unnamed x1 -> x0, blocking collectives: 69.1 us -> none
    unnamed x55 -> x1, local copies, waits for them, and re-layouts: 42.1 us -> 3.5 us
    all_to_all x4 -> x0, starting transfers between devices: 37.4 us -> none  [body(): lax.all_to_all(cycle_rows, ('row', 'col'), split_axis=1, concat_axis=0, t...]
    dot_general x4 -> x0, matrix products: 25.8 us -> none  [body(): jnp.dot(masked, lax.all_gather(coupling, 'row', axis=1, tiled=True), pref...]
    convert_element_type x8 -> x0, local copies, waits for them, and re-layouts: 19.2 us -> none  [body(): cycle_turned = received.T.astype(jnp.float32)]
    all_to_all x8 -> x0, local copies, waits for them, and re-layouts: 16.7 us -> none  [body(): lax.all_to_all(cycle_rows, ('row', 'col'), split_axis=1, concat_axis=0, t...]
  transfers between devices with their start and end apart: 12 -> 0, of which waited for: 5 -> 0; matrix products, arithmetic and copies ran while one was open for 17% -> 0% of each run, Pallas kernels for 0% -> 0%
where the time goes in v1:
time: 131 us
  Pallas kernels  122 us (93%)
  local copies, waits for them, and re-layouts  8.54 us (7%)
    pallas_call x1, Pallas kernels, body(): pl.pallas_call(kernel, out_shape=jax.ShapeDtypeStruct((count, npairs // 1...  122 us
    pallas_call x1, local copies, waits for them, and re-layouts, body(): pl.pallas_call(kernel, out_shape=jax.ShapeDtypeStruct((count, npairs // 1...  5.04 us
    unnamed x1, local copies, waits for them, and re-layouts  3.5 us

profile of v1, /device:TPU:1, one launch (start us, length us, event | category | flops | bytes accessed | tf_op | source)
XLA Modules:
  0.0 130.6 jit_solution(13430824933640320704)
XLA Ops:
  0.0 3.5 %copy.5.b_hbm = bf16[4,576,288]{2,1,0:T(8,128)(2,1)} copy(bf16[4,576,288]{1,2,0:T(8,128)(2,1)} %param.5) | data formatting | bytes 2654208 | tf_op args[1]
  3.5 122.1 %cycle.1 = f32[4,36,4608]{2,1,0:T(8,128)} custom-call(bf16[4,288,576]{2,1,0:T(8,128)(2,1)} %a_hbm.1, bf16[4,576,288]{2,1,0:T(8,128)(2,1)} %copy.5.b_hbm, f32[4,4608]{1,0:T(4,128)} %e_ref.1, s32[4,8]{1,0:T(4,128)} %l_ref.1), custom_call_target="tpu_custom_call" | custom-call | tf_op jit(solution)/shard_map/cycle/pallas_call | solution.py:392
  125.6 5.0 %copy.6 = f32[4,36,4608]{2,0,1:T(4,128)} copy(f32[4,36,4608]{2,1,0:T(8,128)} %cycle.1) | data formatting | bytes 5308416 | tf_op jit(solution)/shard_map/cycle/pallas_call | solution.py:392

commit v2 on v0

v2 whole, which is shorter than its diff:
```python
import functools

import jax
import jax.numpy as jnp
from jax import lax
from jax.experimental import pallas as pl
from jax.experimental.pallas import tpu as pltpu
from jax.sharding import PartitionSpec as P

MESH = pl.DeviceIdType.MESH
BF = jnp.bfloat16
F32 = jnp.float32
I32 = jnp.int32

PARTS = ((0, 80, 48), (80, 64, 32))
PIECES = ((0, 656), (656, 640))

ORDER = (
    ("ready", 1), ("ready", 2), ("relay", 0), ("mul0", 0), ("mul1", 0), ("far0", 0), ("ready", 3), ("relay", 1),
    ("far1", 0), ("near0", 0), ("near1", 0), ("mul0", 1), ("mul1", 1), ("far0", 1), ("relay", 2), ("far1", 1),
    ("near0", 1), ("near1", 1), ("mul0", 2), ("mul1", 2), ("relay", 3), ("sum0", 1), ("far0", 2), ("sum0", 0),
    ("far1", 2), ("near0", 2), ("sum1", 1), ("near1", 2), ("sum1", 0), ("mul0", 3), ("mul1", 3), ("far0", 3),
    ("far1", 3), ("turn", 0), ("near0", 3), ("near1", 3), ("sum0", 2), ("sum1", 2), ("turn", 2), ("sum0", 3),
    ("turn", 1), ("sum1", 3), ("done", 2), ("turn", 3), ("done", 0), ("done", 1), ("done", 3),
)


def nt(a, b):
    return lax.dot_general(a, b, (((1,), (1,)), ((), ())), preferred_element_type=F32)


def nn(a, b):
    return jnp.dot(a, b, preferred_element_type=F32)


def iota(shape, dim):
    return lax.broadcasted_iota(I32, shape, dim)


def natural(j):
    return 2 * (j & 3) + (j >> 2)


def ones_where(hit):
    return hit.astype(F32).astype(BF)


def kernel(
    a_hbm, b_hbm, e_ref, l_ref, o_hbm,
    av, bv, ra, rb, rhs, grem, gremf, lhs, ps, cx, pf, q1, q2, z1, z2, own, db, dx, hm, ht, hr, txm, txs, txr,
    wm, wr, um, tm, tt, pm, qp, ue, fold, sel_m, sel_x, sel_a, s1, s2, mk, er, ob,
    lsem, gos, gor, grs, grr, cs, cr, z1s, z1r, z2s, z2r, hs, hrr, xs, xr, ts, tsr, osem,
):
    row = lax.axis_index("row")
    col = lax.axis_index("col")
    x, y = row // 4, row % 4
    z, c = col // 2, col % 2
    jme = c * 4 + z

    def at(dx, dy, dz, dc):
        return ((x + dx) % 4 * 4 + (y + dy) % 4, (z + dz) % 4 * 2 + (c + dc) % 2)

    def remote(src, dst, ssem, rsem, where):
        return pltpu.make_async_remote_copy(
            src_ref=src, dst_ref=dst, send_sem=ssem, recv_sem=rsem, device_id=where, device_id_type=MESH
        )

    def load(s):
        return (
            pltpu.make_async_copy(a_hbm.at[s], av.at[s], lsem.at[s, 0]),
            pltpu.make_async_copy(b_hbm.at[s], bv.at[s], lsem.at[s, 1]),
        )

    for s in range(4):
        for cp in load(s):
            cp.start()

    def rows_of(v, size):
        return pl.ds(pl.multiple_of(v * size, size), size)

    def gather_own(s, which):
        out = []
        for d, step in ((0, 1), (1, 3)):
            first, size = PIECES[d ^ which]
            rows = pl.ds(first, size)
            blk = ra.at[s, y, rows, :]
            out.append(remote(blk, blk, gos.at[s, d, which, 0], gor.at[s, d, which, 0], at(0, step, 0, 0)))
            blk = rb.at[s, x, rows, :]
            out.append(remote(blk, blk, gos.at[s, d, which, 1], gor.at[s, d, which, 1], at(step, 0, 0, 0)))
        return out

    def gather_relay(s):
        out = []
        for d, step in ((0, 1), (1, 3)):
            first, size = PIECES[d]
            rows = pl.ds(first, size)
            blk = ra.at[s, (y + 4 - step) % 4, rows, :]
            out.append(remote(blk, blk, grs.at[s, d, 0], grr.at[s, d, 0], at(0, step, 0, 0)))
            blk = rb.at[s, (x + 4 - step) % 4, rows, :]
            out.append(remote(blk, blk, grs.at[s, d, 1], grr.at[s, d, 1], at(step, 0, 0, 0)))
        return out

    def swap(s, p):
        rows = pl.ds(*PARTS[p][:2])
        return [remote(ps.at[s, :, rows, :], cx.at[s, :, rows, :], cs.at[s, p], cr.at[s, p], at(0, 0, 0, 1))]

    def zstep1(s, p):
        first, size, up = PARTS[p]
        out = []
        for d, step, rows in ((0, 1, pl.ds(first, up)), (1, 3, pl.ds(first + up, size - up))):
            out.append(remote(
                q1.at[s, rows, :], z1.at[s, rows, :], z1s.at[s, p, d], z1r.at[s, p, d], at(0, 0, step, 0)
            ))
        return out

    def zstep2(s, p):
        rows = pl.ds(*PARTS[p][:2])
        return [
            remote(q2.at[s, d, rows, :], z2.at[s, d, rows, :], z2s.at[s, p, d], z2r.at[s, p, d], at(0, 0, step, 0))
            for d, step in ((0, 1), (1, 3))
        ]

    def here_copies(s):
        out = []
        for d in (1, 2, 3):
            to, yto = at(0, d, 0, 0), (y + d) % 4
            out.append(remote(
                db.at[s, rows_of(yto, 32), :], hm.at[s, y], hs.at[s, d - 1, 0], hrr.at[s, d - 1, 0], to
            ))
            out.append(remote(ht.at[s, yto], hr.at[s, y], hs.at[s, d - 1, 1], hrr.at[s, d - 1, 1], to))
        return out

    def turn_copies(s, p):
        out = []
        for d in (1, 2, 3):
            to, xto = at(d, 0, 0, 0), (x + d) % 4
            if p == 2:
                out.append(remote(txs.at[s, xto], txr.at[s, x], xs.at[s, d - 1, p], xr.at[s, d - 1, p], to))
            else:
                rows = pl.ds(*PARTS[p][:2])
                out.append(remote(
                    dx.at[s, xto, rows, :], txm.at[s, x, rows, :],
                    xs.at[s, d - 1, p], xr.at[s, d - 1, p], to,
                ))
        return out

    def last_copies(s):
        out = []
        for i in (2, 6, 4, 3, 7, 5, 1):
            dz, dc = i // 2, i % 2
            jto = (c + dc) % 2 * 4 + (z + dz) % 4
            out.append(remote(
                um.at[s, jto], tm.at[s, jme], ts.at[s, i - 1], tsr.at[s, i - 1], at(0, 0, dz, dc)
            ))
        return out

    def result_copy(s):
        return pltpu.make_async_copy(ob.at[s], o_hbm.at[:, s, :], osem.at[s])

    def start(copies):
        for cp in copies:
            cp.start()

    def arrive(copies):
        for cp in copies:
            cp.wait_recv()

    def fold_lanes(low, high):
        return jnp.concatenate([low, high], axis=1)

    def ready(s):
        for cp in load(s):
            cp.wait()
        limit = l_ref[s, col]
        masked = jnp.where(iota((288, 576), 1) < limit, av[s].astype(F32), 0.0).astype(BF)
        turned = nn(pm[...], masked)
        b = bv[s]
        for k in range(4):
            ra[s, y, 288 * k:288 * k + 288, :] = turned[:, 128 * k:128 * k + 128].astype(BF)
            rb[s, x, 288 * k:288 * k + 288, :] = b[:, 128 * k:128 * k + 128]
        rest = turned[:, 512:576]
        ra[s, y, 1152:1280, :] = fold_lanes(rest[0:128], rest[128:256]).astype(BF)
        ra[s, y, 1280:1296, :] = fold_lanes(rest[256:272], rest[272:288]).astype(BF)
        rest = b[:, 512:576].astype(F32)
        rb[s, x, 1152:1296, :] = fold_lanes(rest[0:144], rest[144:288]).astype(BF)

    def relay(s):
        arrive(gather_own(s, 0))
        start(gather_relay(s))

        @pl.when(s < 3)
        def _():
            start(gather_own(s + 1, 0))
            start(gather_own(s + 1, 1))

    def unfold(s):
        got = nn(rb[s, :, 1152:1296, :].reshape(576, 128), ue[...]).astype(BF)
        for xx in range(4):
            for k in range(4):
                lanes = slice(128 * k, 128 * k + 128)
                rhs[256 * xx:256 * xx + 256, lanes] = rb[s, xx, 288 * k:288 * k + 256, :]
                rhs[1024 + 32 * xx:1056 + 32 * xx, lanes] = rb[s, xx, 288 * k + 256:288 * k + 288, :]
            low, high = got[144 * xx:144 * xx + 144, 0:256], got[144 * xx:144 * xx + 144, 256:512]
            rhs[256 * xx:256 * xx + 144, 512:768] = low
            rhs[256 * xx + 144:256 * xx + 256, 512:768] = high[0:112]
            rhs[1024 + 32 * xx:1056 + 32 * xx, 512:768] = high[112:144]
        for k in range(4):
            grem[:, 128 * k:128 * k + 128] = nn(
                qp[...], ra[s, :, 288 * k + 256:288 * k + 288, :].reshape(128, 128)
            ).astype(BF)
        gremf[...] = nn(fold[...], ra[s, :, 1280:1296, :].reshape(64, 128)).astype(BF)

    def gather_lhs(s, p, h):
        first, size, _ = PARTS[p]
        lanes = pl.ds(pl.multiple_of(512 + 128 * h, 128), 128)
        lhs[:, pl.ds(pl.multiple_of(640 - 128 * h, 128), 128)] = jnp.zeros((320, 128), BF)
        for zz in range(4):
            at_row = size * zz
            j = h * 4 + zz
            spans = ((0, 0, 32), (1, 0, 32), (2, 0, 16)) if p == 0 else ((2, 16, 16), (3, 0, 32))
            for yy, skip, n in spans:
                for k in range(4):
                    rows = pl.ds(pl.multiple_of(288 * k + 32 * j + skip, 16), n)
                    lhs[at_row:at_row + n, 128 * k:128 * k + 128] = ra[s, yy, rows, :]
                lhs[at_row:at_row + n, lanes] = ra[s, yy, 1152 + 32 * zz + skip:1152 + 32 * zz + skip + n, :]
                at_row += n
            if p == 1:
                lhs[at_row:at_row + 16, 0:512] = grem[rows_of(j, 16), :]
                lhs[at_row:at_row + 16, lanes] = gremf[16 * zz:16 * zz + 16, :]

    def multiply(p, s):
        if p == 0:
            arrive(gather_own(s, 1))
            arrive(gather_relay(s))
            unfold(s)
        first, size, _ = PARTS[p]
        rows = slice(first, first + size)

        def product(h):
            gather_lhs(s, p, h)
            return nt(lhs[0:4 * size, :], rhs[...]).reshape(4, size, 1152)

        ps[s, :, rows, :] = product(1 - c).astype(BF)
        start(swap(s, p))
        pf[:, rows, :] = product(c)

    def each16(first, count, what):
        def one(i, _):
            what(pl.ds(pl.multiple_of(first + i * 16, 16), 16))
            return 0

        lax.fori_loop(0, count // 16, one, 0)

    def here_sum(s, zz, rows):
        return pf[zz, rows, :] + cx[s, zz, rows, :].astype(F32)

    def far(p, s):
        first, size, _ = PARTS[p]
        arrive(swap(s, p))

        def add(rows):
            q1[s, rows, :] = here_sum(s, (z + 2) % 4, rows).astype(BF)

        each16(first, size, add)
        start(zstep1(s, p))

    def near(p, s):
        first, size, up = PARTS[p]
        arrive(zstep1(s, p))
        zup, zdown = (z + 1) % 4, (z + 3) % 4

        def add_up(rows):
            q2[s, 0, rows, :] = (here_sum(s, zup, rows) + z1[s, rows, :].astype(F32)).astype(BF)
            q2[s, 1, rows, :] = here_sum(s, zdown, rows).astype(BF)

        def add_down(rows):
            q2[s, 0, rows, :] = here_sum(s, zup, rows).astype(BF)
            q2[s, 1, rows, :] = (here_sum(s, zdown, rows) + z1[s, rows, :].astype(F32)).astype(BF)

        each16(first, up, add_up)
        each16(first + up, size - up, add_down)
        start(zstep2(s, p))

        def keep(rows):
            own[s, rows, :] = here_sum(s, z, rows)

        each16(first, size, keep)

    def total(p, s):
        first, size, _ = PARTS[p]
        arrive(zstep2(s, p))

        def add(rows):
            v = own[s, rows, :] + z2[s, 0, rows, :].astype(F32) + z2[s, 1, rows, :].astype(F32)
            v = v.astype(BF)
            db[s, rows, :] = v
            for xx in range(4):
                dx[s, xx, rows, :] = v[:, 256 * xx:256 * xx + 256]

        each16(first, size, add)
        start(turn_copies(s, p))
        span = slice(first, first + size)
        txm[s, x, span, :] = dx[s, x, span, :]
        if p == 1:
            tail = db[s, :, 1024:1152].astype(F32)
            for xx in range(4):
                lanes = slice(32 * xx, 32 * xx + 32)
                packed = [tail[48 * g:48 * g + 48, lanes] for g in range(3)]
                packed.append(jnp.zeros((48, 32), F32))
                txs[s, xx] = jnp.concatenate(packed, axis=1).astype(BF)
            start(turn_copies(s, 2))
            txr[s, x] = txs[s, x]
            low = db[s, 128:144, :].astype(F32)
            for yy in range(4):
                mine = low[4 * yy:4 * yy + 4]
                ht[s, yy, :, 0:256] = jnp.concatenate(
                    [mine[:, 256 * xx:256 * xx + 256] for xx in range(4)], axis=0
                ).astype(BF)
                ht[s, yy, :, 256:384] = jnp.concatenate([mine[:, 1024:1152]] * 4, axis=0).astype(BF)
            start(here_copies(s))
            hm[s, y] = db[s, rows_of(y, 32), :]
            hr[s, y] = ht[s, y]

    def turn(s):
        for p in range(3):
            arrive(turn_copies(s, p))
        for xx in range(4):
            packed = txr[s, xx]
            groups = [packed * mk[8 + g:9 + g, 0:128] for g in range(3)]
            wm[128 * xx:128 * xx + 128, 0:256] = txm[s, xx, 0:128, :]
            wm[128 * xx:128 * xx + 48, 256:384] = groups[0]
            wm[128 * xx + 48:128 * xx + 96, 256:384] = groups[1]
            wm[128 * xx + 96:128 * xx + 128, 256:384] = groups[2][0:32]
            wr[64 + 16 * xx:80 + 16 * xx, 0:256] = txm[s, xx, 128:144, :]
            wr[64 + 16 * xx:80 + 16 * xx, 256:384] = groups[2][32:48]
        main = nt(sel_m[...], wm[...]).astype(BF)
        rest = jnp.zeros((128, 128), F32)
        for xx in range(4):
            um[s, :, 32 * xx:32 * xx + 32, :] = main[:, 128 * xx:128 * xx + 128].reshape(8, 32, 128)
            rest += nt(sel_x[xx], wm[128 * xx:128 * xx + 128, :])
        um[s, :, 128:144, :] = rest.astype(BF).reshape(8, 16, 128)
        low, high = wr[64:192, :], wr[0:128, :]
        rest = nt(sel_a[0], low) + nt(sel_a[1], high)
        um[s, :, 144:160, :] = rest.astype(BF).reshape(8, 16, 128)
        every = sel_x[0] + sel_x[1] + sel_x[2] + sel_x[3]
        rest = nt(every, low)
        keep = ((iota((128, 128), 1) >> 4) & 3) == ((iota((128, 128), 0) >> 2) & 3)
        um[s, :, 160:176, :] = jnp.where(keep, rest, 0.0).astype(BF).reshape(8, 16, 128)
        start(last_copies(s))
        tm[s, jme] = um[s, jme]

    def done(s):
        arrive(last_copies(s))
        def across(a, b):
            return jnp.concatenate([tm[s, j, a:b, :] for j in range(8)], axis=1)

        first = across(0, 144)
        packed = across(144, 160)
        second = jnp.concatenate([packed * mk[i:i + 1, :] for i in range(8)] + [across(160, 176)], axis=0)
        for n in range(3):
            cols = slice(384 * n, 384 * n + 384)
            tt[:, cols] = nn(first, s1[:, cols]) + nn(second, s2[:, cols])
        arrive(here_copies(s))
        dev = row * 8 + col
        row_limit = l_ref[s, dev // 16] - (dev % 16) * 36
        row_live = (iota((36, 1), 0) < row_limit).astype(F32)
        row_energy = er[s, 0:36, 0:1]
        lane = iota((1, 1152), 1)
        mains = [hm[s, yy].astype(F32) for yy in range(4)]
        rests = [hr[s, yy].astype(F32) for yy in range(4)]
        for xx in range(4):
            top, low = [], []
            for yy in range(4):
                top += [mains[yy][:, 256 * xx:256 * xx + 256], mains[yy][:, 1024 + 32 * xx:1056 + 32 * xx]]
                four = rests[yy][4 * xx:4 * xx + 4]
                low += [four[:, 0:256], four[:, 256 + 32 * xx:288 + 32 * xx]]
            top = jnp.concatenate(top, axis=1) + tt[32 * xx:32 * xx + 32, :]
            low = jnp.concatenate(low, axis=1) + tt[128 + 4 * xx:132 + 4 * xx, :]
            bound = jnp.where(lane < 576, l_ref[s, 2 * xx], l_ref[s, 2 * xx + 1] + 576)
            col_live = (lane < bound).astype(F32)
            energy = e_ref[pl.ds(s, 1), 1152 * xx:1152 * xx + 1152]
            cols = slice(1152 * xx, 1152 * xx + 1152)
            ob[s, 0:32, cols] = row_live[:32] * col_live * top / (row_energy[:32] + energy)
            ob[s, 32:36, cols] = row_live[32:] * col_live * low / (row_energy[32:] + energy)
        result_copy(s).start()

    def early_constants():
        i = iota((288, 288), 0)
        k = iota((288, 288), 1)
        head = 36 * natural(i >> 5) + (i & 31)
        tail = 36 * natural((i - 256) >> 2) + 32 + (i & 3)
        pm[...] = ones_where(k == jnp.where(i < 256, head, tail))

    def late_constants():
        i = iota((128, 128), 0)
        k = iota((128, 128), 1)
        qp[...] = ones_where(k == 32 * ((i >> 2) & 3) + 4 * (i >> 4) + (i & 3))
        i = iota((64, 64), 0)
        k = iota((64, 64), 1)
        fold[...] = ones_where(k == 16 * ((i >> 2) & 3) + 4 * (i >> 4) + (i & 3))
        i = iota((128, 512), 0)
        k = iota((128, 512), 1)
        lane = k & 127
        half = k >> 8
        hit = ((i >> 6) == half) & ((lane & 63) == (i & 63)) & ((lane >> 6) == ((k >> 7) & 1))
        ue[...] = ones_where(hit)

        def select(q, k):
            return (k == q) | ((k >= 256) & (k < 352) & (((k - 256) & 31) == q - 256))

        def shape3(n):
            return tuple(iota((8, n, 384), d) for d in range(3))

        j, t, k = shape3(32)
        sel_m[...] = ones_where(select(36 * natural(j) + t, k)).reshape(256, 384)
        j, t, k = shape3(16)
        for xx in range(4):
            hit = select(36 * natural(j) + 32 + (t & 3), k) & ((t >> 2) == xx)
            sel_x[xx] = ones_where(hit).reshape(128, 384)
        for h in range(2):
            sel_a[h] = ones_where(select(36 * natural(j) + 16 * h + t, k)).reshape(128, 384)
        wr[...] = jnp.zeros(wr.shape, BF)

        def fill(j, _):
            rows = rows_of(j, 128)
            r = iota((128, 1152), 0)
            k = iota((128, 1152), 1)
            base = 36 * natural(j)
            s1[rows, :] = ones_where(k == 288 * (r >> 5) + base + (r & 31))
            s2[rows, :] = ones_where(k == 288 * ((r >> 2) & 3) + base + 32 + (r & 3))
            return 0

        lax.fori_loop(0, 8, fill, 0)
        r = iota((16, 1024), 0)
        k = iota((16, 1024), 1)
        lane = k & 127
        quarter = ((lane >> 4) & 3) * 2 + (lane >> 6)
        mk[...] = ones_where(((r < 8) & (quarter == r)) | ((r >= 8) & ((lane >> 5) == r - 8)))
        dev = row * 8 + col
        pick = iota((40, 4608), 1) == iota((40, 4608), 0) + dev * 36
        for s in range(4):
            got = jnp.sum(jnp.where(pick, e_ref[s:s + 1, :], 0.0), axis=1, keepdims=True)
            er[s] = jnp.broadcast_to(got, (40, 128))

    early_constants()
    ready(0)
    barrier = pltpu.get_barrier_semaphore()
    partners = [at(d, 0, 0, 0) for d in (1, 2, 3)] + [at(0, d, 0, 0) for d in (1, 2, 3)]
    partners += [at(0, 0, i // 2, i % 2) for i in range(1, 8)]
    for p in partners:
        pl.semaphore_signal(barrier, 1, device_id=p, device_id_type=MESH)
    pl.semaphore_wait(barrier, len(partners))
    start(gather_own(0, 0))
    start(gather_own(0, 1))
    ready(1)
    late_constants()

    work = {
        "ready": ready, "relay": relay, "turn": turn, "done": done,
        "mul0": functools.partial(multiply, 0), "mul1": functools.partial(multiply, 1),
        "far0": functools.partial(far, 0), "far1": functools.partial(far, 1),
        "near0": functools.partial(near, 0), "near1": functools.partial(near, 1),
        "sum0": functools.partial(total, 0), "sum1": functools.partial(total, 1),
    }
    steps = ORDER[1:]

    def one_step(i, _):
        for name, what in work.items():
            places = [(at_step, s) for at_step, (n, s) in enumerate(steps) if n == name]
            now = functools.reduce(jnp.logical_or, [i == at_step for at_step, _ in places])
            s = sum(jnp.where(i == at_step, s, 0) for at_step, s in places)
            pl.when(now)(functools.partial(what, s))
        return 0

    lax.fori_loop(0, len(steps), one_step, 0)

    def drain(s, _):
        copies = gather_own(s, 0) + gather_own(s, 1) + gather_relay(s) + here_copies(s) + last_copies(s)
        for p in range(2):
            copies += swap(s, p) + zstep1(s, p) + zstep2(s, p)
        for p in range(3):
            copies += turn_copies(s, p)
        for cp in copies:
            cp.wait_send()
        result_copy(s).wait()
        return 0

    lax.fori_loop(0, 4, drain, 0)


def body(amplitudes, integrals, pair_energy, block_len):
    bf = lambda *shape: pltpu.VMEM(shape, BF)
    f32 = lambda *shape: pltpu.VMEM(shape, F32)
    dma = lambda *shape: pltpu.SemaphoreType.DMA(shape)
    scratch = [
        bf(4, 288, 576), bf(4, 288, 576),
        bf(4, 4, 1296, 128), bf(4, 4, 1296, 128),
        bf(1152, 768), bf(128, 512), bf(64, 128), bf(320, 768),
        bf(4, 4, 144, 1152), bf(4, 4, 144, 1152), f32(4, 144, 1152),
        bf(4, 144, 1152), bf(4, 2, 144, 1152), bf(4, 144, 1152), bf(4, 2, 144, 1152),
        f32(4, 144, 1152), bf(4, 144, 1152), bf(4, 4, 144, 256),
        bf(4, 4, 32, 1152), bf(4, 4, 16, 384), bf(4, 4, 16, 384),
        bf(4, 4, 144, 256), bf(4, 4, 48, 128), bf(4, 4, 48, 128),
        bf(512, 384), bf(192, 384), bf(4, 8, 176, 128), bf(4, 8, 176, 128), f32(144, 1152),
        bf(288, 288), bf(128, 128), bf(128, 512), bf(64, 64),
        bf(256, 384), bf(4, 128, 384), bf(2, 128, 384),
        bf(1024, 1152), bf(1024, 1152), bf(16, 1024), f32(4, 40, 128), f32(4, 36, 4608),
        dma(4, 2), dma(4, 2, 2, 2), dma(4, 2, 2, 2), dma(4, 2, 2), dma(4, 2, 2), dma(4, 2), dma(4, 2),
        dma(4, 2, 2), dma(4, 2, 2), dma(4, 2, 2), dma(4, 2, 2),
        dma(4, 3, 2), dma(4, 3, 2), dma(4, 3, 3), dma(4, 3, 3), dma(4, 7), dma(4, 7), dma(4),
    ]
    count, npairs = pair_energy.shape
    turned = pl.pallas_call(
        kernel,
        out_shape=jax.ShapeDtypeStruct((npairs // 128, count, npairs), F32),
        in_specs=[
            pl.BlockSpec(memory_space=pl.ANY),
            pl.BlockSpec(memory_space=pl.ANY),
            pl.BlockSpec(memory_space=pltpu.VMEM),
            pl.BlockSpec(memory_space=pltpu.SMEM),
        ],
        out_specs=pl.BlockSpec(memory_space=pl.ANY),
        scratch_shapes=scratch,
        compiler_params=pltpu.CompilerParams(
            collective_id=0, has_side_effects=True, vmem_limit_bytes=63 << 20
        ),
        name="cycle",
    )(amplitudes, jnp.swapaxes(integrals, 1, 2), pair_energy, block_len)
    return jnp.swapaxes(turned, 0, 1)


def solution(mesh):
    return jax.shard_map(
        body,
        mesh=mesh,
        in_specs=(P(None, "row", "col"), P(None, "col", "row"), P(), P()),
        out_specs=P(None, ("row", "col"), None),
        check_vma=False,
    )
```

time: 490 us -> 101 us (0.21); the launches traced: 481 us -> 100 us
  waiting for transfers between devices: 227 us -> 0 us
  Pallas kernels: 0 us -> 97 us
  local copies, waits for them, and re-layouts: 84.9 us -> 3.42 us
  blocking collectives: 69.1 us -> 0 us
  starting transfers between devices: 49.1 us -> 0 us
  matrix products: 25.8 us -> 0 us
  between operations: 14.7 us -> 0.01 us
  other arithmetic: 10.4 us -> 0 us
    all_gather x4 -> x0, waiting for transfers between devices: 224 us -> none  [body(): lax.all_gather(coupling, 'row', axis=1, tiled=True)]
    pallas_call x0 -> x1, Pallas kernels: none -> 97 us  [body(): pl.pallas_call(kernel, out_shape=jax.ShapeDtypeStruct((npairs // 128, cou...]
    unnamed x1 -> x0, blocking collectives: 69.1 us -> none
    unnamed x55 -> x1, local copies, waits for them, and re-layouts: 42.1 us -> 3.42 us
    all_to_all x4 -> x0, starting transfers between devices: 37.4 us -> none  [body(): lax.all_to_all(cycle_rows, ('row', 'col'), split_axis=1, concat_axis=0, t...]
    dot_general x4 -> x0, matrix products: 25.8 us -> none  [body(): jnp.dot(masked, lax.all_gather(coupling, 'row', axis=1, tiled=True), pref...]
    convert_element_type x8 -> x0, local copies, waits for them, and re-layouts: 19.2 us -> none  [body(): cycle_turned = received.T.astype(jnp.float32)]
    all_to_all x8 -> x0, local copies, waits for them, and re-layouts: 16.7 us -> none  [body(): lax.all_to_all(cycle_rows, ('row', 'col'), split_axis=1, concat_axis=0, t...]
  transfers between devices with their start and end apart: 12 -> 0, of which waited for: 5 -> 0; matrix products, arithmetic and copies ran while one was open for 17% -> 0% of each run, Pallas kernels for 0% -> 0%
where the time goes in v2:
time: 101 us; the launch traced here: 100 us
  Pallas kernels  97 us (96%)
  local copies, waits for them, and re-layouts  3.42 us (3%)
    pallas_call x1, Pallas kernels, body(): pl.pallas_call(kernel, out_shape=jax.ShapeDtypeStruct((npairs // 128, cou...  97 us
    unnamed x1, local copies, waits for them, and re-layouts  3.42 us

profile of v2, /device:TPU:1, one launch (start us, length us, event | category | flops | bytes accessed | tf_op | source)
XLA Modules:
  0.0 100.4 jit_solution(16561556446574782183)
XLA Ops:
  0.0 97.0 %cycle.1 = f32[36,4,4608]{2,1,0:T(4,128)} custom-call(bf16[4,288,576]{2,1,0:T(8,128)(2,1)} %a_hbm.1, bf16[4,288,576]{2,1,0:T(8,128)(2,1)} %bitcast.3, f32[4,4608]{1,0:T(4,128)} %e_ref.1, s32[4,8]{1,0:T(4,128)} %l_ref.1), custom_call_target="tpu_custom_call" | custom-call | tf_op jit(solution)/shard_map/cycle/pallas_call | solution.py:513
  97.0 3.4 %copy.6 = f32[4,36,4608]{2,0,1:T(4,128)} copy(f32[4,36,4608]{2,0,1:T(4,128)} %bitcast.2) | data formatting | bytes 5308416

commit v3 on v2

--- a/solution.py
+++ b/solution.py
@@ -15,13 +15,16 @@
 PARTS = ((0, 80, 48), (80, 64, 32))
 PIECES = ((0, 656), (656, 640))
 
+TURNED = ((0, 160), (160, 176))
+
 ORDER = (
-    ("ready", 1), ("ready", 2), ("relay", 0), ("mul0", 0), ("mul1", 0), ("far0", 0), ("ready", 3), ("relay", 1),
-    ("far1", 0), ("near0", 0), ("near1", 0), ("mul0", 1), ("mul1", 1), ("far0", 1), ("relay", 2), ("far1", 1),
-    ("near0", 1), ("near1", 1), ("mul0", 2), ("mul1", 2), ("relay", 3), ("sum0", 1), ("far0", 2), ("sum0", 0),
-    ("far1", 2), ("near0", 2), ("sum1", 1), ("near1", 2), ("sum1", 0), ("mul0", 3), ("mul1", 3), ("far0", 3),
-    ("far1", 3), ("turn", 0), ("near0", 3), ("near1", 3), ("sum0", 2), ("sum1", 2), ("turn", 2), ("sum0", 3),
-    ("turn", 1), ("sum1", 3), ("done", 2), ("turn", 3), ("done", 0), ("done", 1), ("done", 3),
+    ("ready", 1), ("relay", 0), ("ready", 2), ("mul0", 0), ("mul1", 0), ("relay", 1), ("far0", 0), ("ready", 3),
+    ("far1", 0), ("near0", 0), ("mul0", 1), ("far0", 1), ("relay", 2), ("near1", 0), ("mul1", 1), ("far1", 1),
+    ("near0", 1), ("mul0", 2), ("relay", 3), ("far0", 2), ("near1", 1), ("sum0", 0), ("mul1", 2), ("far1", 2),
+    ("near0", 2), ("mul0", 3), ("near1", 2), ("mul1", 3), ("sum1", 0), ("sum0", 1), ("far0", 3), ("sum0", 2),
+    ("far1", 3), ("turn", 0), ("near0", 3), ("here", 0), ("sum1", 1), ("near1", 3), ("drain", 0), ("sum1", 2),
+    ("done", 0), ("turn", 1), ("turn", 2), ("sum0", 3), ("here", 1), ("sum1", 3), ("here", 2), ("turn", 3),
+    ("drain", 1), ("done", 1), ("drain", 2), ("here", 3), ("drain", 3), ("done", 2), ("done", 3),
 )
 
 
@@ -47,18 +50,18 @@
 
 def kernel(
     a_hbm, b_hbm, e_ref, l_ref, o_hbm,
-    av, bv, ra, rb, rhs, grem, gremf, lhs, ps, cx, pf, q1, q2, z1, z2, own, db, dx, hm, ht, hr, txm, txs, txr,
-    wm, wr, um, tm, tt, pm, qp, ue, fold, sel_m, sel_x, sel_a, s1, s2, mk, er, ob,
+    av, bv, ra, rb, rhs, grem, gremf, lhs, ps, cx, pf, q1, q2, z1, z2, own, db, dx, hx, hm, txm,
+    wm, wr, um, tm, sc, pm, qp, ue, fold, sel_m, sel_x, sel_a, s1, s2, mk, er, ob,
     lsem, gos, gor, grs, grr, cs, cr, z1s, z1r, z2s, z2r, hs, hrr, xs, xr, ts, tsr, osem,
 ):
     row = lax.axis_index("row")
     col = lax.axis_index("col")
-    x, y = row // 4, row % 4
-    z, c = col // 2, col % 2
+    x, y = row >> 2, row & 3
+    z, c = col >> 1, col & 1
     jme = c * 4 + z
 
     def at(dx, dy, dz, dc):
-        return ((x + dx) % 4 * 4 + (y + dy) % 4, (z + dz) % 4 * 2 + (c + dc) % 2)
+        return (((x + dx) & 3) * 4 + ((y + dy) & 3), ((z + dz) & 3) * 2 + ((c + dc) & 1))
 
     def remote(src, dst, ssem, rsem, where):
         return pltpu.make_async_remote_copy(
@@ -94,20 +97,30 @@
         for d, step in ((0, 1), (1, 3)):
             first, size = PIECES[d]
             rows = pl.ds(first, size)
-            blk = ra.at[s, (y + 4 - step) % 4, rows, :]
+            blk = ra.at[s, (y + 4 - step) & 3, rows, :]
             out.append(remote(blk, blk, grs.at[s, d, 0], grr.at[s, d, 0], at(0, step, 0, 0)))
-            blk = rb.at[s, (x + 4 - step) % 4, rows, :]
+            blk = rb.at[s, (x + 4 - step) & 3, rows, :]
             out.append(remote(blk, blk, grs.at[s, d, 1], grr.at[s, d, 1], at(step, 0, 0, 0)))
         return out
 
     def swap(s, p):
         rows = pl.ds(*PARTS[p][:2])
-        return [remote(ps.at[s, :, rows, :], cx.at[s, :, rows, :], cs.at[s, p], cr.at[s, p], at(0, 0, 0, 1))]
+        out = []
+        for i, step in enumerate((2, 1, 3, 0)):
+            zz = (z + step) & 3
+            out.append(remote(
+                ps.at[s, zz, rows, :], cx.at[s, zz, rows, :], cs.at[s, p, i], cr.at[s, p, i], at(0, 0, 0, 1)
+            ))
+        return out
+
+    def steps_of(s):
+        odd = s & 1
+        return 1 + 2 * odd, 3 - 2 * odd
 
     def zstep1(s, p):
         first, size, up = PARTS[p]
         out = []
-        for d, step, rows in ((0, 1, pl.ds(first, up)), (1, 3, pl.ds(first + up, size - up))):
+        for d, step, rows in zip((0, 1), steps_of(s), (pl.ds(first, up), pl.ds(first + up, size - up))):
             out.append(remote(
                 q1.at[s, rows, :], z1.at[s, rows, :], z1s.at[s, p, d], z1r.at[s, p, d], at(0, 0, step, 0)
             ))
@@ -117,38 +130,30 @@
         rows = pl.ds(*PARTS[p][:2])
         return [
             remote(q2.at[s, d, rows, :], z2.at[s, d, rows, :], z2s.at[s, p, d], z2r.at[s, p, d], at(0, 0, step, 0))
-            for d, step in ((0, 1), (1, 3))
+            for d, step in zip((0, 1), steps_of(s))
         ]
 
     def here_copies(s):
-        out = []
-        for d in (1, 2, 3):
-            to, yto = at(0, d, 0, 0), (y + d) % 4
-            out.append(remote(
-                db.at[s, rows_of(yto, 32), :], hm.at[s, y], hs.at[s, d - 1, 0], hrr.at[s, d - 1, 0], to
-            ))
-            out.append(remote(ht.at[s, yto], hr.at[s, y], hs.at[s, d - 1, 1], hrr.at[s, d - 1, 1], to))
-        return out
+        return [
+            remote(hx.at[s, (y + d) & 3], hm.at[s, y], hs.at[s, d - 1], hrr.at[s, d - 1], at(0, d, 0, 0))
+            for d in (1, 2, 3)
+        ]
 
     def turn_copies(s, p):
-        out = []
-        for d in (1, 2, 3):
-            to, xto = at(d, 0, 0, 0), (x + d) % 4
-            if p == 2:
-                out.append(remote(txs.at[s, xto], txr.at[s, x], xs.at[s, d - 1, p], xr.at[s, d - 1, p], to))
-            else:
-                rows = pl.ds(*PARTS[p][:2])
-                out.append(remote(
-                    dx.at[s, xto, rows, :], txm.at[s, x, rows, :],
-                    xs.at[s, d - 1, p], xr.at[s, d - 1, p], to,
-                ))
-        return out
+        rows = pl.ds(*TURNED[p])
+        return [
+            remote(
+                dx.at[s, (x + d) & 3, rows, :], txm.at[s, x, rows, :],
+                xs.at[s, d - 1, p], xr.at[s, d - 1, p], at(d, 0, 0, 0),
+            )
+            for d in (1, 2, 3)
+        ]
 
     def last_copies(s):
         out = []
         for i in (2, 6, 4, 3, 7, 5, 1):
             dz, dc = i // 2, i % 2
-            jto = (c + dc) % 2 * 4 + (z + dz) % 4
+            jto = ((c + dc) & 1) * 4 + ((z + dz) & 3)
             out.append(remote(
                 um.at[s, jto], tm.at[s, jme], ts.at[s, i - 1], tsr.at[s, i - 1], at(0, 0, dz, dc)
             ))
@@ -256,18 +261,19 @@
 
     def far(p, s):
         first, size, _ = PARTS[p]
-        arrive(swap(s, p))
+        arrive(swap(s, p)[:1])
 
         def add(rows):
-            q1[s, rows, :] = here_sum(s, (z + 2) % 4, rows).astype(BF)
+            q1[s, rows, :] = here_sum(s, (z + 2) & 3, rows).astype(BF)
 
         each16(first, size, add)
         start(zstep1(s, p))
 
     def near(p, s):
         first, size, up = PARTS[p]
+        arrive(swap(s, p)[1:])
         arrive(zstep1(s, p))
-        zup, zdown = (z + 1) % 4, (z + 3) % 4
+        zup, zdown = ((z + step) & 3 for step in steps_of(s))
 
         def add_up(rows):
             q2[s, 0, rows, :] = (here_sum(s, zup, rows) + z1[s, rows, :].astype(F32)).astype(BF)
@@ -288,50 +294,59 @@
 
     def total(p, s):
         first, size, _ = PARTS[p]
+        base = TURNED[p][0]
         arrive(zstep2(s, p))
 
-        def add(rows):
+        def add(i, _):
+            rows = pl.ds(pl.multiple_of(first + 16 * i, 16), 16)
             v = own[s, rows, :] + z2[s, 0, rows, :].astype(F32) + z2[s, 1, rows, :].astype(F32)
             v = v.astype(BF)
             db[s, rows, :] = v
             for xx in range(4):
-                dx[s, xx, rows, :] = v[:, 256 * xx:256 * xx + 256]
-
-        each16(first, size, add)
-        start(turn_copies(s, p))
-        span = slice(first, first + size)
-        txm[s, x, span, :] = dx[s, x, span, :]
+                for k in range(2):
+                    to = pl.ds(pl.multiple_of(base + size * k + 16 * i, 16), 16)
+                    dx[s, xx, to, :] = v[:, 256 * xx + 128 * k:256 * xx + 128 * k + 128]
+            return 0
+
+        lax.fori_loop(0, size // 16, add, 0)
         if p == 1:
             tail = db[s, :, 1024:1152].astype(F32)
             for xx in range(4):
                 lanes = slice(32 * xx, 32 * xx + 32)
                 packed = [tail[48 * g:48 * g + 48, lanes] for g in range(3)]
                 packed.append(jnp.zeros((48, 32), F32))
-                txs[s, xx] = jnp.concatenate(packed, axis=1).astype(BF)
-            start(turn_copies(s, 2))
-            txr[s, x] = txs[s, x]
-            low = db[s, 128:144, :].astype(F32)
+                dx[s, xx, 288:336, :] = jnp.concatenate(packed, axis=1).astype(BF)
+        start(turn_copies(s, p))
+        span = slice(base, base + TURNED[p][1])
+        txm[s, x, span, :] = dx[s, x, span, :]
+        if p == 1:
             for yy in range(4):
-                mine = low[4 * yy:4 * yy + 4]
-                ht[s, yy, :, 0:256] = jnp.concatenate(
-                    [mine[:, 256 * xx:256 * xx + 256] for xx in range(4)], axis=0
-                ).astype(BF)
-                ht[s, yy, :, 256:384] = jnp.concatenate([mine[:, 1024:1152]] * 4, axis=0).astype(BF)
+                for k in range(9):
+                    hx[s, yy, 32 * k:32 * k + 32, :] = db[s, 32 * yy:32 * yy + 32, 128 * k:128 * k + 128]
+                mine = db[s, 128:144, :].astype(F32)[4 * yy:4 * yy + 4]
+                for k in range(3):
+                    lanes = [128 * k + 256 * xx if k < 2 else 1024 for xx in range(4)]
+                    hx[s, yy, 288 + 16 * k:304 + 16 * k, :] = jnp.concatenate(
+                        [mine[:, i:i + 128] for i in lanes], axis=0
+                    ).astype(BF)
             start(here_copies(s))
-            hm[s, y] = db[s, rows_of(y, 32), :]
-            hr[s, y] = ht[s, y]
+            hm[s, y] = hx[s, y]
 
     def turn(s):
-        for p in range(3):
+        for p in range(2):
             arrive(turn_copies(s, p))
         for xx in range(4):
-            packed = txr[s, xx]
+            packed = txm[s, xx, 288:336, :]
             groups = [packed * mk[8 + g:9 + g, 0:128] for g in range(3)]
-            wm[128 * xx:128 * xx + 128, 0:256] = txm[s, xx, 0:128, :]
-            wm[128 * xx:128 * xx + 48, 256:384] = groups[0]
-            wm[128 * xx + 48:128 * xx + 96, 256:384] = groups[1]
-            wm[128 * xx + 96:128 * xx + 128, 256:384] = groups[2][0:32]
-            wr[64 + 16 * xx:80 + 16 * xx, 0:256] = txm[s, xx, 128:144, :]
+            at_row = 128 * xx
+            for k in range(2):
+                lanes = slice(128 * k, 128 * k + 128)
+                wm[at_row:at_row + 80, lanes] = txm[s, xx, 80 * k:80 * k + 80, :]
+                wm[at_row + 80:at_row + 128, lanes] = txm[s, xx, 160 + 64 * k:208 + 64 * k, :]
+                wr[64 + 16 * xx:80 + 16 * xx, lanes] = txm[s, xx, 208 + 64 * k:224 + 64 * k, :]
+            wm[at_row:at_row + 48, 256:384] = groups[0]
+            wm[at_row + 48:at_row + 96, 256:384] = groups[1]
+            wm[at_row + 96:at_row + 128, 256:384] = groups[2][0:32]
             wr[64 + 16 * xx:80 + 16 * xx, 256:384] = groups[2][32:48]
         main = nt(sel_m[...], wm[...]).astype(BF)
         rest = jnp.zeros((128, 128), F32)
@@ -349,8 +364,33 @@
         start(last_copies(s))
         tm[s, jme] = um[s, jme]
 
+    def here(s):
+        arrive(here_copies(s))
+        slot = s & 1
+        dev = row * 8 + col
+        row_limit = l_ref[s, dev >> 4] - (dev & 15) * 36
+        row_live = (iota((36, 1), 0) < row_limit).astype(F32)
+        row_energy = er[s, 0:36, 0:1]
+        lane = iota((1, 1152), 1)
+        tiles = [[hm[s, yy, 32 * k:32 * k + 32, :].astype(F32) for k in range(9)] for yy in range(4)]
+        rests = [[hm[s, yy, 288 + 16 * k:304 + 16 * k, :].astype(F32) for k in range(3)] for yy in range(4)]
+        for xx in range(4):
+            top, low = [], []
+            for yy in range(4):
+                last = slice(32 * xx, 32 * xx + 32)
+                top += [tiles[yy][2 * xx], tiles[yy][2 * xx + 1], tiles[yy][8][:, last]]
+                low += [v[4 * xx:4 * xx + 4] for v in rests[yy][:2]] + [rests[yy][2][4 * xx:4 * xx + 4, last]]
+            cols = slice(1152 * xx, 1152 * xx + 1152)
+            ob[s, 0:32, cols] = jnp.concatenate(top, axis=1)
+            ob[s, 32:36, cols] = jnp.concatenate(low, axis=1)
+            bound = jnp.where(lane < 576, l_ref[s, 2 * xx], l_ref[s, 2 * xx + 1] + 576)
+            col_live = (lane < bound).astype(F32)
+            sc[slot, :, cols] = row_live * col_live / (row_energy + e_ref[pl.ds(s, 1), cols])
+
     def done(s):
+        slot = s & 1
         arrive(last_copies(s))
+
         def across(a, b):
             return jnp.concatenate([tm[s, j, a:b, :] for j in range(8)], axis=1)
 
@@ -359,29 +399,11 @@
         second = jnp.concatenate([packed * mk[i:i + 1, :] for i in range(8)] + [across(160, 176)], axis=0)
         for n in range(3):
             cols = slice(384 * n, 384 * n + 384)
-            tt[:, cols] = nn(first, s1[:, cols]) + nn(second, s2[:, cols])
-        arrive(here_copies(s))
-        dev = row * 8 + col
-        row_limit = l_ref[s, dev // 16] - (dev % 16) * 36
-        row_live = (iota((36, 1), 0) < row_limit).astype(F32)
-        row_energy = er[s, 0:36, 0:1]
-        lane = iota((1, 1152), 1)
-        mains = [hm[s, yy].astype(F32) for yy in range(4)]
-        rests = [hr[s, yy].astype(F32) for yy in range(4)]
-        for xx in range(4):
-            top, low = [], []
-            for yy in range(4):
-                top += [mains[yy][:, 256 * xx:256 * xx + 256], mains[yy][:, 1024 + 32 * xx:1056 + 32 * xx]]
-                four = rests[yy][4 * xx:4 * xx + 4]
-                low += [four[:, 0:256], four[:, 256 + 32 * xx:288 + 32 * xx]]
-            top = jnp.concatenate(top, axis=1) + tt[32 * xx:32 * xx + 32, :]
-            low = jnp.concatenate(low, axis=1) + tt[128 + 4 * xx:132 + 4 * xx, :]
-            bound = jnp.where(lane < 576, l_ref[s, 2 * xx], l_ref[s, 2 * xx + 1] + 576)
-            col_live = (lane < bound).astype(F32)
-            energy = e_ref[pl.ds(s, 1), 1152 * xx:1152 * xx + 1152]
-            cols = slice(1152 * xx, 1152 * xx + 1152)
-            ob[s, 0:32, cols] = row_live[:32] * col_live * top / (row_energy[:32] + energy)
-            ob[s, 32:36, cols] = row_live[32:] * col_live * low / (row_energy[32:] + energy)
+            got = nn(first, s1[:, cols]) + nn(second, s2[:, cols])
+            for xx in range(4):
+                cols = slice(1152 * xx + 384 * n, 1152 * xx + 384 * n + 384)
+                ob[s, 0:32, cols] = (ob[s, 0:32, cols] + got[32 * xx:32 * xx + 32]) * sc[slot, 0:32, cols]
+                ob[s, 32:36, cols] = (ob[s, 32:36, cols] + got[128 + 4 * xx:132 + 4 * xx]) * sc[slot, 32:36, cols]
         result_copy(s).start()
 
     def early_constants():
@@ -455,8 +477,20 @@
     ready(1)
     late_constants()
 
+    def drain(s):
+        copies = gather_own(s, 0) + gather_own(s, 1) + gather_relay(s) + here_copies(s)
+        for p in range(2):
+            copies += swap(s, p) + zstep1(s, p) + zstep2(s, p) + turn_copies(s, p)
+        for cp in copies:
+            cp.wait_send()
+
+        @pl.when(s < 3)
+        def _():
+            for cp in last_copies(s):
+                cp.wait_send()
+
     work = {
-        "ready": ready, "relay": relay, "turn": turn, "done": done,
+        "ready": ready, "relay": relay, "turn": turn, "here": here, "done": done, "drain": drain,
         "mul0": functools.partial(multiply, 0), "mul1": functools.partial(multiply, 1),
         "far0": functools.partial(far, 0), "far1": functools.partial(far, 1),
         "near0": functools.partial(near, 0), "near1": functools.partial(near, 1),
@@ -474,18 +508,10 @@
 
     lax.fori_loop(0, len(steps), one_step, 0)
 
-    def drain(s, _):
-        copies = gather_own(s, 0) + gather_own(s, 1) + gather_relay(s) + here_copies(s) + last_copies(s)
-        for p in range(2):
-            copies += swap(s, p) + zstep1(s, p) + zstep2(s, p)
-        for p in range(3):
-            copies += turn_copies(s, p)
-        for cp in copies:
-            cp.wait_send()
+    for cp in last_copies(3):
+        cp.wait_send()
+    for s in range(4):
         result_copy(s).wait()
-        return 0
-
-    lax.fori_loop(0, 4, drain, 0)
 
 
 def body(amplitudes, integrals, pair_energy, block_len):
@@ -498,31 +524,30 @@
         bf(1152, 768), bf(128, 512), bf(64, 128), bf(320, 768),
         bf(4, 4, 144, 1152), bf(4, 4, 144, 1152), f32(4, 144, 1152),
         bf(4, 144, 1152), bf(4, 2, 144, 1152), bf(4, 144, 1152), bf(4, 2, 144, 1152),
-        f32(4, 144, 1152), bf(4, 144, 1152), bf(4, 4, 144, 256),
-        bf(4, 4, 32, 1152), bf(4, 4, 16, 384), bf(4, 4, 16, 384),
-        bf(4, 4, 144, 256), bf(4, 4, 48, 128), bf(4, 4, 48, 128),
-        bf(512, 384), bf(192, 384), bf(4, 8, 176, 128), bf(4, 8, 176, 128), f32(144, 1152),
+        f32(4, 144, 1152), bf(4, 144, 1152), bf(4, 4, 336, 128),
+        bf(4, 4, 336, 128), bf(4, 4, 336, 128), bf(4, 4, 336, 128),
+        bf(512, 384), bf(192, 384), bf(4, 8, 176, 128), bf(4, 8, 176, 128), f32(2, 36, 4608),
         bf(288, 288), bf(128, 128), bf(128, 512), bf(64, 64),
         bf(256, 384), bf(4, 128, 384), bf(2, 128, 384),
         bf(1024, 1152), bf(1024, 1152), bf(16, 1024), f32(4, 40, 128), f32(4, 36, 4608),
-        dma(4, 2), dma(4, 2, 2, 2), dma(4, 2, 2, 2), dma(4, 2, 2), dma(4, 2, 2), dma(4, 2), dma(4, 2),
+        dma(4, 2), dma(4, 2, 2, 2), dma(4, 2, 2, 2), dma(4, 2, 2), dma(4, 2, 2), dma(4, 2, 4), dma(4, 2, 4),
         dma(4, 2, 2), dma(4, 2, 2), dma(4, 2, 2), dma(4, 2, 2),
-        dma(4, 3, 2), dma(4, 3, 2), dma(4, 3, 3), dma(4, 3, 3), dma(4, 7), dma(4, 7), dma(4),
+        dma(4, 3), dma(4, 3), dma(4, 3, 2), dma(4, 3, 2), dma(4, 7), dma(4, 7), dma(4),
     ]
     count, npairs = pair_energy.shape
     turned = pl.pallas_call(
         kernel,
-        out_shape=jax.ShapeDtypeStruct((npairs // 128, count, npairs), F32),
+        out_shape=pltpu.VMEM((npairs // 128, count, npairs), F32),
         in_specs=[
             pl.BlockSpec(memory_space=pl.ANY),
             pl.BlockSpec(memory_space=pl.ANY),
             pl.BlockSpec(memory_space=pltpu.VMEM),
             pl.BlockSpec(memory_space=pltpu.SMEM),
         ],
-        out_specs=pl.BlockSpec(memory_space=pl.ANY),
+        out_specs=pl.BlockSpec(memory_space=pltpu.VMEM),
         scratch_shapes=scratch,
         compiler_params=pltpu.CompilerParams(
-            collective_id=0, has_side_effects=True, vmem_limit_bytes=63 << 20
+            collective_id=0, has_side_effects=True, vmem_limit_bytes=60 << 20
         ),
         name="cycle",
     )(amplitudes, jnp.swapaxes(integrals, 1, 2), pair_energy, block_len)

time: 101 us -> 97.3 us (0.963)
  local copies, waits for them, and re-layouts: 3.42 us -> 1.5 us
  Pallas kernels: 97 us -> 95.6 us
    unnamed x1, local copies, waits for them, and re-layouts: 3.42 us -> 1.5 us
    pallas_call x1, Pallas kernels: 97 us -> 95.6 us  [body(): pl.pallas_call(kernel, out_shape=pltpu.VMEM((npairs // 128, count, npairs...]
where the time goes in v3:
time: 97.3 us; the launch traced here: 97.1 us
  Pallas kernels  95.6 us (98%)
  local copies, waits for them, and re-layouts  1.5 us (2%)
    pallas_call x1, Pallas kernels, body(): pl.pallas_call(kernel, out_shape=pltpu.VMEM((npairs // 128, count, npairs...  95.6 us

profile of v3, /device:TPU:1, one launch (start us, length us, event | category | flops | bytes accessed | tf_op | source)
XLA Modules:
  0.0 97.1 jit_solution(2009058102015404609)
XLA Ops:
  0.0 95.6 %cycle.1 = f32[36,4,4608]{2,1,0:T(4,128)S(1)} custom-call(bf16[4,288,576]{2,1,0:T(8,128)(2,1)} %a_hbm.1, bf16[4,288,576]{2,1,0:T(8,128)(2,1)} %bitcast.3, f32[4,4608]{1,0:T(4,128)} %e_ref.1, s32[4,8]{1,0:T(4,128)} %l_ref.1), custom_call_target="tpu_custom_call" | custom-call | tf_op jit(solution)/shard_map/cycle/pallas_call | solution.py:538
  95.6 1.5 %copy.6 = f32[4,36,4608]{2,0,1:T(4,128)} copy(f32[4,36,4608]{2,0,1:T(4,128)S(1)} %bitcast.2) | data formatting | bytes 5308416

commit v4 on v3

--- a/solution.py
+++ b/solution.py
@@ -49,9 +49,9 @@
 
 
 def kernel(
-    a_hbm, b_hbm, e_ref, l_ref, o_hbm,
+    a_hbm, b_hbm, e_ref, l_ref, o_ref,
     av, bv, ra, rb, rhs, grem, gremf, lhs, ps, cx, pf, q1, q2, z1, z2, own, db, dx, hx, hm, txm,
-    wm, wr, um, tm, sc, pm, qp, ue, fold, sel_m, sel_x, sel_a, s1, s2, mk, er, ob,
+    wm, wr, um, tm, sc, pm, qp, ue, fold, sel_m, sel_x, sel_a, s12, mk, er, ob,
     lsem, gos, gor, grs, grr, cs, cr, z1s, z1r, z2s, z2r, hs, hrr, xs, xr, ts, tsr, osem,
 ):
     row = lax.axis_index("row")
@@ -74,9 +74,14 @@
             pltpu.make_async_copy(b_hbm.at[s], bv.at[s], lsem.at[s, 1]),
         )
 
-    for s in range(4):
-        for cp in load(s):
-            cp.start()
+    for cp in load(0):
+        cp.start()
+
+    barrier = pltpu.get_barrier_semaphore()
+    partners = [at(d, 0, 0, 0) for d in (1, 2, 3)] + [at(0, d, 0, 0) for d in (1, 2, 3)]
+    partners += [at(0, 0, i // 2, i % 2) for i in range(1, 8)]
+    for p in partners:
+        pl.semaphore_signal(barrier, 1, device_id=p, device_id_type=MESH)
 
     def rows_of(v, size):
         return pl.ds(pl.multiple_of(v * size, size), size)
@@ -159,8 +164,9 @@
             ))
         return out
 
-    def result_copy(s):
-        return pltpu.make_async_copy(ob.at[s], o_hbm.at[:, s, :], osem.at[s])
+    def result_copy(s, xx):
+        cols = pl.ds(1152 * xx, 1152)
+        return pltpu.make_async_copy(ob.at[s, :, cols], o_ref.at[:, s, cols], osem.at[s, xx])
 
     def start(copies):
         for cp in copies:
@@ -198,17 +204,24 @@
             start(gather_own(s + 1, 0))
             start(gather_own(s + 1, 1))
 
+    def unfold_block(s, xx):
+        got = nn(rb[s, xx, 1152:1296, :], ue[...]).astype(BF)
+        low, high = got[:, 0:256], got[:, 256:512]
+
+        def main(first, size):
+            return pl.ds(pl.multiple_of(256 * xx + first, 16), size)
+
+        rest = pl.ds(pl.multiple_of(1024 + 32 * xx, 32), 32)
+        for k in range(4):
+            lanes = slice(128 * k, 128 * k + 128)
+            rhs[main(0, 256), lanes] = rb[s, xx, 288 * k:288 * k + 256, :]
+            rhs[rest, lanes] = rb[s, xx, 288 * k + 256:288 * k + 288, :]
+        rhs[main(0, 144), 512:768] = low
+        rhs[main(144, 112), 512:768] = high[0:112]
+        rhs[rest, 512:768] = high[112:144]
+
     def unfold(s):
-        got = nn(rb[s, :, 1152:1296, :].reshape(576, 128), ue[...]).astype(BF)
-        for xx in range(4):
-            for k in range(4):
-                lanes = slice(128 * k, 128 * k + 128)
-                rhs[256 * xx:256 * xx + 256, lanes] = rb[s, xx, 288 * k:288 * k + 256, :]
-                rhs[1024 + 32 * xx:1056 + 32 * xx, lanes] = rb[s, xx, 288 * k + 256:288 * k + 288, :]
-            low, high = got[144 * xx:144 * xx + 144, 0:256], got[144 * xx:144 * xx + 144, 256:512]
-            rhs[256 * xx:256 * xx + 144, 512:768] = low
-            rhs[256 * xx + 144:256 * xx + 256, 512:768] = high[0:112]
-            rhs[1024 + 32 * xx:1056 + 32 * xx, 512:768] = high[112:144]
+        unfold_block(s, (x + 2) & 3)
         for k in range(4):
             grem[:, 128 * k:128 * k + 128] = nn(
                 qp[...], ra[s, :, 288 * k + 256:288 * k + 288, :].reshape(128, 128)
@@ -236,6 +249,8 @@
     def multiply(p, s):
         if p == 0:
             arrive(gather_own(s, 1))
+            for d in (0, 1, 3):
+                unfold_block(s, (x + d) & 3)
             arrive(gather_relay(s))
             unfold(s)
         first, size, _ = PARTS[p]
@@ -397,14 +412,12 @@
         first = across(0, 144)
         packed = across(144, 160)
         second = jnp.concatenate([packed * mk[i:i + 1, :] for i in range(8)] + [across(160, 176)], axis=0)
-        for n in range(3):
-            cols = slice(384 * n, 384 * n + 384)
-            got = nn(first, s1[:, cols]) + nn(second, s2[:, cols])
-            for xx in range(4):
-                cols = slice(1152 * xx + 384 * n, 1152 * xx + 384 * n + 384)
-                ob[s, 0:32, cols] = (ob[s, 0:32, cols] + got[32 * xx:32 * xx + 32]) * sc[slot, 0:32, cols]
-                ob[s, 32:36, cols] = (ob[s, 32:36, cols] + got[128 + 4 * xx:132 + 4 * xx]) * sc[slot, 32:36, cols]
-        result_copy(s).start()
+        got = nn(jnp.concatenate([first, second], axis=1), s12[...])
+        for xx in range(4):
+            cols = slice(1152 * xx, 1152 * xx + 1152)
+            ob[s, 0:32, cols] = (ob[s, 0:32, cols] + got[32 * xx:32 * xx + 32]) * sc[slot, 0:32, cols]
+            ob[s, 32:36, cols] = (ob[s, 32:36, cols] + got[128 + 4 * xx:132 + 4 * xx]) * sc[slot, 32:36, cols]
+            result_copy(s, xx).start()
 
     def early_constants():
         i = iota((288, 288), 0)
@@ -448,8 +461,9 @@
             r = iota((128, 1152), 0)
             k = iota((128, 1152), 1)
             base = 36 * natural(j)
-            s1[rows, :] = ones_where(k == 288 * (r >> 5) + base + (r & 31))
-            s2[rows, :] = ones_where(k == 288 * ((r >> 2) & 3) + base + 32 + (r & 3))
+            s12[rows, :] = ones_where(k == 288 * (r >> 5) + base + (r & 31))
+            rows = pl.ds(pl.multiple_of(128 * j + 1024, 128), 128)
+            s12[rows, :] = ones_where(k == 288 * ((r >> 2) & 3) + base + 32 + (r & 3))
             return 0
 
         lax.fori_loop(0, 8, fill, 0)
@@ -466,11 +480,9 @@
 
     early_constants()
     ready(0)
-    barrier = pltpu.get_barrier_semaphore()
-    partners = [at(d, 0, 0, 0) for d in (1, 2, 3)] + [at(0, d, 0, 0) for d in (1, 2, 3)]
-    partners += [at(0, 0, i // 2, i % 2) for i in range(1, 8)]
-    for p in partners:
-        pl.semaphore_signal(barrier, 1, device_id=p, device_id_type=MESH)
+    for s in range(1, 4):
+        for cp in load(s):
+            cp.start()
     pl.semaphore_wait(barrier, len(partners))
     start(gather_own(0, 0))
     start(gather_own(0, 1))
@@ -511,7 +523,8 @@
     for cp in last_copies(3):
         cp.wait_send()
     for s in range(4):
-        result_copy(s).wait()
+        for xx in range(4):
+            result_copy(s, xx).wait()
 
 
 def body(amplitudes, integrals, pair_energy, block_len):
@@ -529,10 +542,10 @@
         bf(512, 384), bf(192, 384), bf(4, 8, 176, 128), bf(4, 8, 176, 128), f32(2, 36, 4608),
         bf(288, 288), bf(128, 128), bf(128, 512), bf(64, 64),
         bf(256, 384), bf(4, 128, 384), bf(2, 128, 384),
-        bf(1024, 1152), bf(1024, 1152), bf(16, 1024), f32(4, 40, 128), f32(4, 36, 4608),
+        bf(2048, 1152), bf(16, 1024), f32(4, 40, 128), f32(4, 36, 4608),
         dma(4, 2), dma(4, 2, 2, 2), dma(4, 2, 2, 2), dma(4, 2, 2), dma(4, 2, 2), dma(4, 2, 4), dma(4, 2, 4),
         dma(4, 2, 2), dma(4, 2, 2), dma(4, 2, 2), dma(4, 2, 2),
-        dma(4, 3), dma(4, 3), dma(4, 3, 2), dma(4, 3, 2), dma(4, 7), dma(4, 7), dma(4),
+        dma(4, 3), dma(4, 3), dma(4, 3, 2), dma(4, 3, 2), dma(4, 7), dma(4, 7), dma(4, 4),
     ]
     count, npairs = pair_energy.shape
     turned = pl.pallas_call(

time: 97.3 us -> 95.8 us (0.985)
  Pallas kernels: 95.6 us -> 94.1 us
    pallas_call x1, Pallas kernels: 95.6 us -> 94.1 us  [body(): pl.pallas_call(kernel, out_shape=pltpu.VMEM((npairs // 128, count, npairs...]
where the time goes in v4:
time: 95.8 us; the launch traced here: 95.6 us
  Pallas kernels  94.1 us (98%)
  local copies, waits for them, and re-layouts  1.5 us (2%)
    pallas_call x1, Pallas kernels, body(): pl.pallas_call(kernel, out_shape=pltpu.VMEM((npairs // 128, count, npairs...  94.1 us

profile of v4, /device:TPU:1, one launch (start us, length us, event | category | flops | bytes accessed | tf_op | source)
XLA Modules:
  0.0 95.6 jit_solution(11885629857668232388)
XLA Ops:
  0.0 94.1 %cycle.1 = f32[36,4,4608]{2,1,0:T(4,128)S(1)} custom-call(bf16[4,288,576]{2,1,0:T(8,128)(2,1)} %a_hbm.1, bf16[4,288,576]{2,1,0:T(8,128)(2,1)} %bitcast.3, f32[4,4608]{1,0:T(4,128)} %e_ref.1, s32[4,8]{1,0:T(4,128)} %l_ref.1), custom_call_target="tpu_custom_call" | custom-call | tf_op jit(solution)/shard_map/cycle/pallas_call | solution.py:551
  94.1 1.5 %copy.6 = f32[4,36,4608]{2,0,1:T(4,128)} copy(f32[4,36,4608]{2,0,1:T(4,128)S(1)} %bitcast.2) | data formatting | bytes 5308416

commit v5 on v4

--- a/solution.py
+++ b/solution.py
@@ -12,19 +12,22 @@
 F32 = jnp.float32
 I32 = jnp.int32
 
-PARTS = ((0, 80, 48), (80, 64, 32))
+PARTS = ((0, 96, 48, 0, 768), (0, 96, 48, 768, 384), (96, 48, 32, 0, 1152))
+SLOT = {1: 1, 3: 2, 2: 3}
 PIECES = ((0, 656), (656, 640))
 
-TURNED = ((0, 160), (160, 176))
+TURNED = ((0, 192), (192, 144))
 
 ORDER = (
-    ("ready", 1), ("relay", 0), ("ready", 2), ("mul0", 0), ("mul1", 0), ("relay", 1), ("far0", 0), ("ready", 3),
-    ("far1", 0), ("near0", 0), ("mul0", 1), ("far0", 1), ("relay", 2), ("near1", 0), ("mul1", 1), ("far1", 1),
-    ("near0", 1), ("mul0", 2), ("relay", 3), ("far0", 2), ("near1", 1), ("sum0", 0), ("mul1", 2), ("far1", 2),
-    ("near0", 2), ("mul0", 3), ("near1", 2), ("mul1", 3), ("sum1", 0), ("sum0", 1), ("far0", 3), ("sum0", 2),
-    ("far1", 3), ("turn", 0), ("near0", 3), ("here", 0), ("sum1", 1), ("near1", 3), ("drain", 0), ("sum1", 2),
-    ("done", 0), ("turn", 1), ("turn", 2), ("sum0", 3), ("here", 1), ("sum1", 3), ("here", 2), ("turn", 3),
-    ("drain", 1), ("done", 1), ("drain", 2), ("here", 3), ("drain", 3), ("done", 2), ("done", 3),
+    ("ready", 1), ("relay", 0), ("ready", 2), ("mul0", 0), ("far0", 0), ("mul1", 0), ("far1", 0), ("near0", 0),
+    ("mul2", 0), ("relay", 1), ("near1", 0), ("far2", 0), ("mul0", 1), ("far0", 1), ("near2", 0), ("mul1", 1),
+    ("far1", 1), ("ready", 3), ("near0", 1), ("mul2", 1), ("relay", 2), ("far2", 1), ("near1", 1), ("mul0", 2),
+    ("far0", 2), ("near2", 1), ("mul1", 2), ("far1", 2), ("near0", 2), ("relay", 3), ("mul2", 2), ("far2", 2),
+    ("sum0", 1), ("near1", 2), ("mul0", 3), ("far0", 3), ("sum0", 0), ("near2", 2), ("mul1", 3), ("sum1", 0),
+    ("far1", 3), ("sum1", 1), ("sum2", 0), ("near0", 3), ("mul2", 3), ("sum2", 1), ("far2", 3), ("near1", 3),
+    ("turn", 0), ("sum0", 2), ("sum1", 2), ("drain", 0), ("near2", 3), ("sum2", 2), ("turn", 1), ("here", 1),
+    ("sum0", 3), ("here", 0), ("sum1", 3), ("done", 0), ("turn", 2), ("sum2", 3), ("turn", 3), ("here", 2),
+    ("drain", 3), ("done", 1), ("here", 3), ("done", 2), ("drain", 2), ("drain", 1), ("done", 3),
 )
 
 
@@ -108,13 +111,17 @@
             out.append(remote(blk, blk, grs.at[s, d, 1], grr.at[s, d, 1], at(step, 0, 0, 0)))
         return out
 
+    def spans(p):
+        first, size, _, lane, width = PARTS[p]
+        return pl.ds(first, size), pl.ds(lane, width)
+
     def swap(s, p):
-        rows = pl.ds(*PARTS[p][:2])
+        rows, lanes = spans(p)
         out = []
         for i, step in enumerate((2, 1, 3, 0)):
             zz = (z + step) & 3
             out.append(remote(
-                ps.at[s, zz, rows, :], cx.at[s, zz, rows, :], cs.at[s, p, i], cr.at[s, p, i], at(0, 0, 0, 1)
+                ps.at[s, zz, rows, lanes], cx.at[s, zz, rows, lanes], cs.at[s, p, i], cr.at[s, p, i], at(0, 0, 0, 1)
             ))
         return out
 
@@ -123,18 +130,22 @@
         return 1 + 2 * odd, 3 - 2 * odd
 
     def zstep1(s, p):
-        first, size, up = PARTS[p]
+        first, size, up, _, _ = PARTS[p]
+        lanes = spans(p)[1]
         out = []
         for d, step, rows in zip((0, 1), steps_of(s), (pl.ds(first, up), pl.ds(first + up, size - up))):
             out.append(remote(
-                q1.at[s, rows, :], z1.at[s, rows, :], z1s.at[s, p, d], z1r.at[s, p, d], at(0, 0, step, 0)
+                q1.at[s, rows, lanes], z1.at[s, rows, lanes], z1s.at[s, p, d], z1r.at[s, p, d], at(0, 0, step, 0)
             ))
         return out
 
     def zstep2(s, p):
-        rows = pl.ds(*PARTS[p][:2])
+        rows, lanes = spans(p)
         return [
-            remote(q2.at[s, d, rows, :], z2.at[s, d, rows, :], z2s.at[s, p, d], z2r.at[s, p, d], at(0, 0, step, 0))
+            remote(
+                q2.at[s, d, rows, lanes], z2.at[s, d, rows, lanes],
+                z2s.at[s, p, d], z2r.at[s, p, d], at(0, 0, step, 0),
+            )
             for d, step in zip((0, 1), steps_of(s))
         ]
 
@@ -144,14 +155,14 @@
             for d in (1, 2, 3)
         ]
 
-    def turn_copies(s, p):
-        rows = pl.ds(*TURNED[p])
+    def turn_copies(s, piece, targets=(1, 3, 2)):
+        rows = pl.ds(*TURNED[piece])
         return [
             remote(
-                dx.at[s, (x + d) & 3, rows, :], txm.at[s, x, rows, :],
-                xs.at[s, d - 1, p], xr.at[s, d - 1, p], at(d, 0, 0, 0),
+                dx.at[s, SLOT[d], rows, :], txm.at[s, x, rows, :],
+                xs.at[s, d - 1, piece], xr.at[s, d - 1, piece], at(d, 0, 0, 0),
             )
-            for d in (1, 2, 3)
+            for d in targets
         ]
 
     def last_copies(s):
@@ -204,65 +215,70 @@
             start(gather_own(s + 1, 0))
             start(gather_own(s + 1, 1))
 
-    def unfold_block(s, xx):
+    def near_to(v, slot):
+        return (v + (slot ^ (slot >> 1))) & 3
+
+    def unfold(s, slot):
+        xx = near_to(x, slot)
         got = nn(rb[s, xx, 1152:1296, :], ue[...]).astype(BF)
         low, high = got[:, 0:256], got[:, 256:512]
-
-        def main(first, size):
-            return pl.ds(pl.multiple_of(256 * xx + first, 16), size)
-
-        rest = pl.ds(pl.multiple_of(1024 + 32 * xx, 32), 32)
+        main, rest = 256 * slot, slice(1024 + 32 * slot, 1056 + 32 * slot)
         for k in range(4):
             lanes = slice(128 * k, 128 * k + 128)
-            rhs[main(0, 256), lanes] = rb[s, xx, 288 * k:288 * k + 256, :]
+            rhs[main:main + 256, lanes] = rb[s, xx, 288 * k:288 * k + 256, :]
             rhs[rest, lanes] = rb[s, xx, 288 * k + 256:288 * k + 288, :]
-        rhs[main(0, 144), 512:768] = low
-        rhs[main(144, 112), 512:768] = high[0:112]
+        rhs[main:main + 144, 512:768] = low
+        rhs[main + 144:main + 256, 512:768] = high[0:112]
         rhs[rest, 512:768] = high[112:144]
 
-    def unfold(s):
-        unfold_block(s, (x + 2) & 3)
+    def last_rows(s):
         for k in range(4):
             grem[:, 128 * k:128 * k + 128] = nn(
                 qp[...], ra[s, :, 288 * k + 256:288 * k + 288, :].reshape(128, 128)
             ).astype(BF)
         gremf[...] = nn(fold[...], ra[s, :, 1280:1296, :].reshape(64, 128)).astype(BF)
 
-    def gather_lhs(s, p, h):
-        first, size, _ = PARTS[p]
+    def gather_lhs(s, slots, h, i):
         lanes = pl.ds(pl.multiple_of(512 + 128 * h, 128), 128)
-        lhs[:, pl.ds(pl.multiple_of(640 - 128 * h, 128), 128)] = jnp.zeros((320, 128), BF)
+        lhs[i, :, pl.ds(pl.multiple_of(640 - 128 * h, 128), 128)] = jnp.zeros((384, 128), BF)
+        at_row = 0
         for zz in range(4):
-            at_row = size * zz
             j = h * 4 + zz
-            spans = ((0, 0, 32), (1, 0, 32), (2, 0, 16)) if p == 0 else ((2, 16, 16), (3, 0, 32))
-            for yy, skip, n in spans:
+            for slot in slots:
+                yy = near_to(y, slot)
                 for k in range(4):
-                    rows = pl.ds(pl.multiple_of(288 * k + 32 * j + skip, 16), n)
-                    lhs[at_row:at_row + n, 128 * k:128 * k + 128] = ra[s, yy, rows, :]
-                lhs[at_row:at_row + n, lanes] = ra[s, yy, 1152 + 32 * zz + skip:1152 + 32 * zz + skip + n, :]
-                at_row += n
-            if p == 1:
-                lhs[at_row:at_row + 16, 0:512] = grem[rows_of(j, 16), :]
-                lhs[at_row:at_row + 16, lanes] = gremf[16 * zz:16 * zz + 16, :]
+                    rows = pl.ds(pl.multiple_of(288 * k + 32 * j, 16), 32)
+                    lhs[i, at_row:at_row + 32, 128 * k:128 * k + 128] = ra[s, yy, rows, :]
+                lhs[i, at_row:at_row + 32, lanes] = ra[s, yy, 1152 + 32 * zz:1184 + 32 * zz, :]
+                at_row += 32
+            if slots == (3,):
+                lhs[i, at_row:at_row + 16, 0:512] = grem[rows_of(j, 16), :]
+                lhs[i, at_row:at_row + 16, lanes] = gremf[16 * zz:16 * zz + 16, :]
+                at_row += 16
 
     def multiply(p, s):
         if p == 0:
             arrive(gather_own(s, 1))
-            for d in (0, 1, 3):
-                unfold_block(s, (x + d) & 3)
+            for slot in range(3):
+                unfold(s, slot)
+            for i, h in ((0, 1 - c), (1, c)):
+                gather_lhs(s, (0, 1, 2), h, i)
+        if p == 1:
             arrive(gather_relay(s))
-            unfold(s)
-        first, size, _ = PARTS[p]
-        rows = slice(first, first + size)
-
-        def product(h):
-            gather_lhs(s, p, h)
-            return nt(lhs[0:4 * size, :], rhs[...]).reshape(4, size, 1152)
-
-        ps[s, :, rows, :] = product(1 - c).astype(BF)
+            unfold(s, 3)
+        if p == 2:
+            last_rows(s)
+            for i, h in ((0, 1 - c), (1, c)):
+                gather_lhs(s, (3,), h, i)
+        first, size, _, lane, width = PARTS[p]
+        rows, lanes = slice(first, first + size), slice(lane, lane + width)
+
+        def product(i):
+            return nt(lhs[i, 0:4 * size, :], rhs[lanes, :]).reshape(4, size, width)
+
+        ps[s, :, rows, lanes] = product(0).astype(BF)
         start(swap(s, p))
-        pf[:, rows, :] = product(c)
+        pf[:, rows, lanes] = product(1)
 
     def each16(first, count, what):
         def one(i, _):
@@ -271,79 +287,91 @@
 
         lax.fori_loop(0, count // 16, one, 0)
 
-    def here_sum(s, zz, rows):
-        return pf[zz, rows, :] + cx[s, zz, rows, :].astype(F32)
+    def here_sum(s, zz, rows, lanes):
+        return pf[zz, rows, lanes] + cx[s, zz, rows, lanes].astype(F32)
 
     def far(p, s):
-        first, size, _ = PARTS[p]
+        first, size, _, lane, width = PARTS[p]
+        lanes = slice(lane, lane + width)
         arrive(swap(s, p)[:1])
 
         def add(rows):
-            q1[s, rows, :] = here_sum(s, (z + 2) & 3, rows).astype(BF)
+            q1[s, rows, lanes] = here_sum(s, (z + 2) & 3, rows, lanes).astype(BF)
 
         each16(first, size, add)
         start(zstep1(s, p))
 
     def near(p, s):
-        first, size, up = PARTS[p]
+        first, size, up, lane, width = PARTS[p]
+        lanes = slice(lane, lane + width)
         arrive(swap(s, p)[1:])
         arrive(zstep1(s, p))
         zup, zdown = ((z + step) & 3 for step in steps_of(s))
 
         def add_up(rows):
-            q2[s, 0, rows, :] = (here_sum(s, zup, rows) + z1[s, rows, :].astype(F32)).astype(BF)
-            q2[s, 1, rows, :] = here_sum(s, zdown, rows).astype(BF)
+            q2[s, 0, rows, lanes] = (here_sum(s, zup, rows, lanes) + z1[s, rows, lanes].astype(F32)).astype(BF)
+            q2[s, 1, rows, lanes] = here_sum(s, zdown, rows, lanes).astype(BF)
 
         def add_down(rows):
-            q2[s, 0, rows, :] = here_sum(s, zup, rows).astype(BF)
-            q2[s, 1, rows, :] = (here_sum(s, zdown, rows) + z1[s, rows, :].astype(F32)).astype(BF)
+            q2[s, 0, rows, lanes] = here_sum(s, zup, rows, lanes).astype(BF)
+            q2[s, 1, rows, lanes] = (here_sum(s, zdown, rows, lanes) + z1[s, rows, lanes].astype(F32)).astype(BF)
 
         each16(first, up, add_up)
         each16(first + up, size - up, add_down)
         start(zstep2(s, p))
 
         def keep(rows):
-            own[s, rows, :] = here_sum(s, z, rows)
+            own[s, rows, lanes] = here_sum(s, z, rows, lanes)
 
         each16(first, size, keep)
 
     def total(p, s):
-        first, size, _ = PARTS[p]
-        base = TURNED[p][0]
+        first, size, _, lane, width = PARTS[p]
+        lanes = slice(lane, lane + width)
+        base = 0 if p < 2 else TURNED[1][0]
+        slots = ((0, 1, 2), (3,), (0, 1, 2, 3))[p]
         arrive(zstep2(s, p))
 
         def add(i, _):
             rows = pl.ds(pl.multiple_of(first + 16 * i, 16), 16)
-            v = own[s, rows, :] + z2[s, 0, rows, :].astype(F32) + z2[s, 1, rows, :].astype(F32)
+            v = own[s, rows, lanes] + z2[s, 0, rows, lanes].astype(F32) + z2[s, 1, rows, lanes].astype(F32)
             v = v.astype(BF)
-            db[s, rows, :] = v
-            for xx in range(4):
+            db[s, rows, lanes] = v
+            for slot in slots:
                 for k in range(2):
                     to = pl.ds(pl.multiple_of(base + size * k + 16 * i, 16), 16)
-                    dx[s, xx, to, :] = v[:, 256 * xx + 128 * k:256 * xx + 128 * k + 128]
+                    at_lane = 256 * slot + 128 * k - lane
+                    dx[s, slot, to, :] = v[:, at_lane:at_lane + 128]
             return 0
 
         lax.fori_loop(0, size // 16, add, 0)
+        if p == 0:
+            start(turn_copies(s, 0, (1, 3)))
+            txm[s, x, 0:192, :] = dx[s, 0, 0:192, :]
         if p == 1:
+            start(turn_copies(s, 0, (2,)))
+        if p == 2:
             tail = db[s, :, 1024:1152].astype(F32)
-            for xx in range(4):
-                lanes = slice(32 * xx, 32 * xx + 32)
-                packed = [tail[48 * g:48 * g + 48, lanes] for g in range(3)]
+            for slot in range(4):
+                cut = slice(32 * slot, 32 * slot + 32)
+                packed = [tail[48 * g:48 * g + 48, cut] for g in range(3)]
                 packed.append(jnp.zeros((48, 32), F32))
-                dx[s, xx, 288:336, :] = jnp.concatenate(packed, axis=1).astype(BF)
-        start(turn_copies(s, p))
-        span = slice(base, base + TURNED[p][1])
-        txm[s, x, span, :] = dx[s, x, span, :]
-        if p == 1:
+                dx[s, slot, 288:336, :] = jnp.concatenate(packed, axis=1).astype(BF)
+            start(turn_copies(s, 1))
+            txm[s, x, 192:336, :] = dx[s, 0, 192:336, :]
+            low = db[s, 128:144, :].astype(F32)
             for yy in range(4):
+                mine = low[4 * yy:4 * yy + 4]
+                for k in range(3):
+                    at_lanes = [128 * k + 256 * slot if k < 2 else 1024 for slot in range(4)]
+                    hx[s, yy, 288 + 16 * k:304 + 16 * k, :] = jnp.concatenate(
+                        [mine[:, i:i + 128] for i in at_lanes], axis=0
+                    ).astype(BF)
+            for slot in range(4):
                 for k in range(9):
-                    hx[s, yy, 32 * k:32 * k + 32, :] = db[s, 32 * yy:32 * yy + 32, 128 * k:128 * k + 128]
-                mine = db[s, 128:144, :].astype(F32)[4 * yy:4 * yy + 4]
-                for k in range(3):
-                    lanes = [128 * k + 256 * xx if k < 2 else 1024 for xx in range(4)]
-                    hx[s, yy, 288 + 16 * k:304 + 16 * k, :] = jnp.concatenate(
-                        [mine[:, i:i + 128] for i in lanes], axis=0
-                    ).astype(BF)
+                    hx[s, near_to(y, slot), 32 * k:32 * k + 32, :] = db[
+                        s, 32 * slot:32 * slot + 32, 128 * k:128 * k + 128
+                    ]
             start(here_copies(s))
             hm[s, y] = hx[s, y]
 
@@ -356,9 +384,9 @@
             at_row = 128 * xx
             for k in range(2):
                 lanes = slice(128 * k, 128 * k + 128)
-                wm[at_row:at_row + 80, lanes] = txm[s, xx, 80 * k:80 * k + 80, :]
-                wm[at_row + 80:at_row + 128, lanes] = txm[s, xx, 160 + 64 * k:208 + 64 * k, :]
-                wr[64 + 16 * xx:80 + 16 * xx, lanes] = txm[s, xx, 208 + 64 * k:224 + 64 * k, :]
+                wm[at_row:at_row + 96, lanes] = txm[s, xx, 96 * k:96 * k + 96, :]
+                wm[at_row + 96:at_row + 128, lanes] = txm[s, xx, 192 + 48 * k:224 + 48 * k, :]
+                wr[64 + 16 * xx:80 + 16 * xx, lanes] = txm[s, xx, 224 + 48 * k:240 + 48 * k, :]
             wm[at_row:at_row + 48, 256:384] = groups[0]
             wm[at_row + 48:at_row + 96, 256:384] = groups[1]
             wm[at_row + 96:at_row + 128, 256:384] = groups[2][0:32]
@@ -395,10 +423,11 @@
                 last = slice(32 * xx, 32 * xx + 32)
                 top += [tiles[yy][2 * xx], tiles[yy][2 * xx + 1], tiles[yy][8][:, last]]
                 low += [v[4 * xx:4 * xx + 4] for v in rests[yy][:2]] + [rests[yy][2][4 * xx:4 * xx + 4, last]]
-            cols = slice(1152 * xx, 1152 * xx + 1152)
+            xto = near_to(x, xx)
+            cols = pl.ds(pl.multiple_of(1152 * xto, 1152), 1152)
             ob[s, 0:32, cols] = jnp.concatenate(top, axis=1)
             ob[s, 32:36, cols] = jnp.concatenate(low, axis=1)
-            bound = jnp.where(lane < 576, l_ref[s, 2 * xx], l_ref[s, 2 * xx + 1] + 576)
+            bound = jnp.where(lane < 576, l_ref[s, 2 * xto], l_ref[s, 2 * xto + 1] + 576)
             col_live = (lane < bound).astype(F32)
             sc[slot, :, cols] = row_live * col_live / (row_energy + e_ref[pl.ds(s, 1), cols])
 
@@ -461,7 +490,7 @@
             r = iota((128, 1152), 0)
             k = iota((128, 1152), 1)
             base = 36 * natural(j)
-            s12[rows, :] = ones_where(k == 288 * (r >> 5) + base + (r & 31))
+            s12[rows, :] = ones_where(k == 288 * near_to(y, r >> 5) + base + (r & 31))
             rows = pl.ds(pl.multiple_of(128 * j + 1024, 128), 128)
             s12[rows, :] = ones_where(k == 288 * ((r >> 2) & 3) + base + 32 + (r & 3))
             return 0
@@ -492,7 +521,9 @@
     def drain(s):
         copies = gather_own(s, 0) + gather_own(s, 1) + gather_relay(s) + here_copies(s)
         for p in range(2):
-            copies += swap(s, p) + zstep1(s, p) + zstep2(s, p) + turn_copies(s, p)
+            copies += turn_copies(s, p)
+        for p in range(3):
+            copies += swap(s, p) + zstep1(s, p) + zstep2(s, p)
         for cp in copies:
             cp.wait_send()
 
@@ -503,11 +534,10 @@
 
     work = {
         "ready": ready, "relay": relay, "turn": turn, "here": here, "done": done, "drain": drain,
-        "mul0": functools.partial(multiply, 0), "mul1": functools.partial(multiply, 1),
-        "far0": functools.partial(far, 0), "far1": functools.partial(far, 1),
-        "near0": functools.partial(near, 0), "near1": functools.partial(near, 1),
-        "sum0": functools.partial(total, 0), "sum1": functools.partial(total, 1),
     }
+    for p in range(3):
+        for name, what in (("mul", multiply), ("far", far), ("near", near), ("sum", total)):
+            work[name + str(p)] = functools.partial(what, p)
     steps = ORDER[1:]
 
     def one_step(i, _):
@@ -534,7 +564,7 @@
     scratch = [
         bf(4, 288, 576), bf(4, 288, 576),
         bf(4, 4, 1296, 128), bf(4, 4, 1296, 128),
-        bf(1152, 768), bf(128, 512), bf(64, 128), bf(320, 768),
+        bf(1152, 768), bf(128, 512), bf(64, 128), bf(2, 384, 768),
         bf(4, 4, 144, 1152), bf(4, 4, 144, 1152), f32(4, 144, 1152),
         bf(4, 144, 1152), bf(4, 2, 144, 1152), bf(4, 144, 1152), bf(4, 2, 144, 1152),
         f32(4, 144, 1152), bf(4, 144, 1152), bf(4, 4, 336, 128),
@@ -543,8 +573,8 @@
         bf(288, 288), bf(128, 128), bf(128, 512), bf(64, 64),
         bf(256, 384), bf(4, 128, 384), bf(2, 128, 384),
         bf(2048, 1152), bf(16, 1024), f32(4, 40, 128), f32(4, 36, 4608),
-        dma(4, 2), dma(4, 2, 2, 2), dma(4, 2, 2, 2), dma(4, 2, 2), dma(4, 2, 2), dma(4, 2, 4), dma(4, 2, 4),
-        dma(4, 2, 2), dma(4, 2, 2), dma(4, 2, 2), dma(4, 2, 2),
+        dma(4, 2), dma(4, 2, 2, 2), dma(4, 2, 2, 2), dma(4, 2, 2), dma(4, 2, 2), dma(4, 3, 4), dma(4, 3, 4),
+        dma(4, 3, 2), dma(4, 3, 2), dma(4, 3, 2), dma(4, 3, 2),
         dma(4, 3), dma(4, 3), dma(4, 3, 2), dma(4, 3, 2), dma(4, 7), dma(4, 7), dma(4, 4),
     ]
     count, npairs = pair_energy.shape
@@ -560,7 +590,7 @@
         out_specs=pl.BlockSpec(memory_space=pltpu.VMEM),
         scratch_shapes=scratch,
         compiler_params=pltpu.CompilerParams(
-            collective_id=0, has_side_effects=True, vmem_limit_bytes=60 << 20
+            collective_id=0, has_side_effects=True, vmem_limit_bytes=121 << 19
         ),
         name="cycle",
     )(amplitudes, jnp.swapaxes(integrals, 1, 2), pair_energy, block_len)

time: 95.8 us -> 94.9 us (level)
  Pallas kernels: 94.1 us -> 92.4 us
    pallas_call x1, Pallas kernels: 94.1 us -> 92.4 us  [body(): pl.pallas_call(kernel, out_shape=pltpu.VMEM((npairs // 128, count, npairs...]
where the time goes in v5:
time: 94.9 us; the launch traced here: 93.9 us
  Pallas kernels  92.4 us (97%)
  local copies, waits for them, and re-layouts  1.5 us (2%)
    pallas_call x1, Pallas kernels, body(): pl.pallas_call(kernel, out_shape=pltpu.VMEM((npairs // 128, count, npairs...  92.4 us

profile of v5, /device:TPU:1, one launch (start us, length us, event | category | flops | bytes accessed | tf_op | source)
XLA Modules:
  0.0 93.9 jit_solution(17606367481376310996)
XLA Ops:
  0.0 92.4 %cycle.1 = f32[36,4,4608]{2,1,0:T(4,128)S(1)} custom-call(bf16[4,288,576]{2,1,0:T(8,128)(2,1)} %a_hbm.1, bf16[4,288,576]{2,1,0:T(8,128)(2,1)} %bitcast.3, f32[4,4608]{1,0:T(4,128)} %e_ref.1, s32[4,8]{1,0:T(4,128)} %l_ref.1), custom_call_target="tpu_custom_call" | custom-call | tf_op jit(solution)/shard_map/cycle/pallas_call | solution.py:581
  92.4 1.5 %copy.6 = f32[4,36,4608]{2,0,1:T(4,128)} copy(f32[4,36,4608]{2,0,1:T(4,128)S(1)} %bitcast.2) | data formatting | bytes 5308416
